TPU v7x, 32 devices: a whole 2x2x4 slice. The times are simulated.
32 devices in a mesh: blk: 16 (over z, y, x), chan: 2 (over core).
Axes of the slice: x: 2, y: 2, z: 4, core: 2. Of those that a mesh axis runs over, the one named last changes fastest.
Arguments:
- inputs: bfloat16 [128, 64, 512], P('chan', 'blk'), may hold values from -6 to 6
- w_first: bfloat16 [3, 3, 128, 128], P(None, None, 'chan'), may hold values from -0.1875 to 0.1875
- w_second: bfloat16 [3, 3, 128, 128], P(None, None, 'chan'), may hold values from -0.1875 to 0.1875
- w_third: bfloat16 [3, 3, 256, 128], P(None, None, 'chan'), may hold values from -0.1875 to 0.1875
- cotangent: bfloat16 [256, 32, 256], P('chan', 'blk'), may hold values from -6 to 6
- mirror: int32 [16], P('blk'), may hold values from 0 to 1
Outputs:
- grad_inputs: bfloat16 [128, 64, 512], P('chan', 'blk')
- grad_first: float32 [3, 3, 128, 128], P(None, None, 'chan')
- grad_second: float32 [3, 3, 128, 128], P(None, None, 'chan')
- grad_third: float32 [3, 3, 256, 128], P(None, None, 'chan')
Inputs may be any that keep to these rules, and one draw needn't show every extreme that they name: `mirror`: 1 marks a tile whose columns are stored in reverse order, 0 a tile stored in the cycle's order.
All inputs are finite; a program needn't handle non-finite values.
Results may differ from a plain program's by a relative error of at most 0.024.
Values may be sent and summed in bfloat16 or wider, within the bound.
No kernel may reach another device: no remote copies, remote signals or barrier semaphores. Data moves between devices by JAX's collectives and lax.ppermute only.
A program may use at most 64 MiB of HBM per device.

v0:
```python
import functools
import math

import jax
import jax.numpy as jnp
from jax import lax
from jax.experimental import pallas as pl
from jax.experimental.pallas import tpu as pltpu
from jax.sharding import PartitionSpec as P

BF = jnp.bfloat16
F32 = jnp.float32
ROOT = math.sqrt(2.0 / math.pi)
CUBIC = 0.044715


def dot(a, b):
    return jnp.dot(a, b, preferred_element_type=F32)


def dot_t(a, b):
    return lax.dot_general(a, b, (((1,), (1,)), ((), ())), preferred_element_type=F32)


def moved_right(v):
    lane = lax.broadcasted_iota(jnp.int32, v.shape, 1)
    return jnp.where(lane == 0, 0.0, pltpu.roll(v, 1, 1))


def moved_left(v):
    lane = lax.broadcasted_iota(jnp.int32, v.shape, 1)
    width = v.shape[1]
    return jnp.where(lane == width - 1, 0.0, pltpu.roll(v, width - 1, 1))


def gelu_parts(v):
    square = v * v
    t = jnp.tanh(v * (ROOT + (ROOT * CUBIC) * square))
    half = 0.5 * v
    return half + half * t, 0.5 + 0.5 * t + half * (1.0 - t * t) * (ROOT + (3.0 * ROOT * CUBIC) * square)


def either(me, own, other):
    return jnp.where(me == 0, own, other), jnp.where(me == 0, other, own)


def put_weights(me, own1, other1, own2, other2, own3, other3, wb1, wb2, wt2, wt1, wt3e, wt3o):
    c = own1.shape[1]
    h = c // 2
    stack = 4 * c
    for out in (wb1, wb2, wt2, wt1, wt3e, wt3o):
        out[...] = jnp.zeros_like(out)
    for a in range(3):
        for b in range(3):
            tap = a * 3 + b
            at = pl.ds(tap * h, h)
            first = jnp.concatenate(either(me, own1[at, :], other1[at, :]), axis=0)
            second = jnp.concatenate(either(me, own2[at, :], other2[at, :]), axis=0)
            for par in range(2):
                at = pl.ds(a * stack + (b + par) * c, c)
                wb1[pl.ds(par * c, c), at] = first
                wb2[pl.ds(par * c, c), at] = second
            turned = second.T
            first_turned = first.T
            half_turned = jnp.where(me == 0, first_turned[:h], first_turned[h:])
            for par in range(2):
                at = pl.ds((2 - a) * stack + (2 - b + par) * c, c)
                wt2[pl.ds(par * c, c), at] = turned
                wt1[pl.ds(par * h, h), at] = half_turned
            at = pl.ds(tap * c, c)
            third = jnp.concatenate([w.T for w in either(me, own3[at, :], other3[at, :])], axis=1)
            par = 0 if b == 1 else 1
            side = 1 if b == 0 else 0
            if a == 1:
                wt3e[pl.ds(par * c, c), pl.ds(side * 2 * c, 2 * c)] = third
            else:
                back = 0 if a == 2 else 1
                wt3o[pl.ds(par * c, c), pl.ds((back * 2 + side) * 2 * c, 2 * c)] = third


def put_stack(ref, base, row):
    c = row.shape[0] // 2
    even, odd = row[:c], row[c:]
    ref[pl.ds(base, c), :] = moved_right(odd).astype(BF)
    ref[pl.ds(base + c, 2 * c), :] = row.astype(BF)
    ref[pl.ds(base + 3 * c, c), :] = moved_left(even).astype(BF)


def run(tasks):
    waiting = None
    for task in tasks:
        value = task[0]()
        if waiting:
            waiting[0](waiting[1])
        waiting = (task[1], value)
    waiting[0](waiting[1])


def deal(pieces, grads, tile):
    for k, piece in enumerate(pieces):
        at = piece_at(tile, k)
        base = 0
        for grad in grads:
            size = grad.shape[0] // 4
            piece[pl.ds(base, size), :] = grad[pl.ds(pl.multiple_of(at * size, 16), size), :]
            base += size


def put_input(ref, base, at, row):
    h, m = row.shape[0], row.shape[1] // 2
    even, odd = row[:, :m], row[:, m:]
    blocks = (moved_right(odd.astype(F32)).astype(BF), even, odd, moved_left(even.astype(F32)).astype(BF))
    for k, block in enumerate(blocks):
        ref[pl.ds(pl.multiple_of(base + k * 2 * h + at * h, h), h), :] = block


def put_cotangent(ref, base, at, row):
    h, m = row.shape[0], row.shape[1] // 2
    for k in range(2):
        block = row[:, k * m : (k + 1) * m]
        to = base + at * 2 * h + k * h
        ref[pl.ds(pl.multiple_of(to, h), h), :] = block
        ref[pl.ds(pl.multiple_of(to + 4 * h, h), h), :] = moved_left(block.astype(F32)).astype(BF)


def put_outer(tx, tu, at, around):
    stack = tx.shape[0] // 3
    for k in range(3):
        put_input(tx, k * stack, at, around[k])
    put_cotangent(tu, 0, at, around[3])


def outer_kernel(core, around, tx, tu):
    put_outer(tx, tu, core[0], around)


def taps(r, first, last):
    mine = [a for a in range(3) if first <= r + a - 1 < last]
    return mine, [a for a in range(3) if a not in mine]


def inner_kernel(
    core, own, other, w1, other1, w2, other2, w3, other3,
    wb1, wb2, wt2, wt1, wt3e, wt3o, tx, tu, th1, dz1, g2, part1, part2,
):
    me = core[0]
    c = wb1.shape[0] // 2
    stack = 4 * c
    rows = own.shape[0] // 3 * 2

    def part_dot(weight, ref, first, last, r):
        mine = taps(r, first, last)[0]
        some = ref[pl.ds((r + mine[0] - 1 - first) * stack, len(mine) * stack), :]
        return dot(weight[:, pl.ds(mine[0] * stack, len(mine) * stack)], some)

    def part_use(out, k, value):
        out[pl.ds(k * 2 * c, 2 * c), :] = value

    put_weights(me, w1, other1, w2, other2, w3, other3, wb1, wb2, wt2, wt1, wt3e, wt3o)
    for r in range(rows):
        put_input(tx, r * stack, me, own[r])
        put_input(tx, r * stack, 1 - me, other[r])
    for r in range(rows // 2):
        put_cotangent(tu, r * stack, me, own[rows + r])
        put_cotangent(tu, r * stack, 1 - me, other[rows + r])

    def first_dot(r):
        return dot(wb1[...], tx[pl.ds((r - 1) * stack, 3 * stack), :])

    def first_use(r, z):
        act, slope = gelu_parts(z)
        put_stack(th1, (r - 1) * stack, act)
        dz1[pl.ds((r - 1) * 2 * c, 2 * c), :] = slope

    def third_dot(r):
        if r % 2 == 0:
            return dot(wt3e[...], tu[pl.ds(r // 2 * stack, stack), :])
        return dot(wt3o[...], tu[pl.ds(r // 2 * stack, 2 * stack), :])

    def third_use(r, back):
        g2[pl.ds(r * 2 * c, 2 * c), :] = back

    z1 = [(functools.partial(first_dot, r), functools.partial(first_use, r)) for r in range(1, rows - 1)]
    back = [(functools.partial(third_dot, r), functools.partial(third_use, r)) for r in range(rows - 1)]
    outer = (-1, 0, rows - 1, rows)
    first = [(functools.partial(part_dot, wb1, tx, 0, rows, r), functools.partial(part_use, part1, k)) for k, r in enumerate(outer)]
    second = [(functools.partial(part_dot, wb2, th1, 1, rows - 1, r), functools.partial(part_use, part2, r)) for r in range(rows)]
    run(z1 + back + first + second)


def main_kernel(
    core, _txb, _tub, _txa, _tua, before, after, wb1, wb2, wt2, wt3e, wt3o, txi, tui, th1i, dz1i, g2i, part1, part2,
    p0, p1, p2, p3, td1, txb, tub, txa, tua, th1o, dz1o, dz2, th2, td2, s2, s1, dw1, dw2, dw3,
):
    me = core[0]
    c = wb1.shape[0] // 2
    h = c // 2
    m = td1.shape[1]
    stack = 4 * c
    rows = td1.shape[0] // stack - 4

    def input_at(r):
        if 0 <= r < rows:
            return txi, r * stack
        return (txb, (r + 3) * stack) if r < 0 else (txa, (r - rows) * stack)

    def first_at(r):
        if 1 <= r < rows - 1:
            return th1i, (r - 1) * stack
        return th1o, (r + 2 if r < 1 else r - rows + 4) * stack

    def cotangent_at(r):
        if 0 <= r < rows // 2:
            return tui, r * stack
        return tub if r < 0 else tua, 0

    def window(at, first, count):
        places = [at(r) for r in range(first, first + count)]
        return jnp.concatenate([ref[pl.ds(base, stack), :] for ref, base in places], axis=0)

    def own_channels(ref, index, out, r):
        for par in range(2):
            at = pl.multiple_of(index * stack + (1 + par) * c + me * h, h)
            out[par, pl.ds((rows + 1 - r) * h, h), :] = ref[pl.ds(at, h), :]

    def rest_dot(weight, at, first, last, part, k, r):
        others = taps(r, first, last)[1]
        some = window(at, r + others[0] - 1, len(others))
        value = dot(weight[:, pl.ds(others[0] * stack, len(others) * stack)], some)
        return value if len(others) == 3 else value + part[pl.ds(k * 2 * c, 2 * c), :]

    def first_dot(r):
        return rest_dot(wb1, input_at, 0, rows, part1, r + 1 if r < 1 else r - rows + 3, r)

    def first_use(r, z):
        act, slope = gelu_parts(z)
        ref, base = first_at(r)
        put_stack(ref, base, act)
        if r in (0, rows - 1):
            dz1o[pl.ds((r > 0) * 2 * c, 2 * c), :] = slope

    def second_dot(r):
        return rest_dot(wb2, first_at, 1, rows - 1, part2, r, r)

    def second_use(r, z):
        act, slope = gelu_parts(z)
        k = r + 1
        dz2[pl.ds(k * 2 * c, 2 * c), :] = slope
        if r < rows:
            th2[pl.ds(k * 3 * c, c), :] = moved_right(act[c:]).astype(BF)
            th2[pl.ds(k * 3 * c + c, 2 * c), :] = act.astype(BF)

    def third_dot(r):
        if 0 <= r < rows - 1:
            return None
        if r % 2 == 0:
            return dot(wt3e[...], window(cotangent_at, r // 2, 1))
        return dot(wt3o[...], window(cotangent_at, (r - 1) // 2 if r > 0 else -1, 2))

    def third_use(r, back):
        if back is None:
            back = g2i[pl.ds(r * 2 * c, 2 * c), :]
        k = r + 1
        put_stack(td2, k * stack, back * dz2[pl.ds(k * 2 * c, 2 * c), :])
        if 0 <= r < rows:
            own_channels(td2, k, s2, r)

    def back_dot(r):
        return dot(wt2[...], td2[pl.ds(r * stack, 3 * stack), :])

    def back_use(r, back):
        if 0 < r < rows - 1:
            slope = dz1i[pl.ds((r - 1) * 2 * c, 2 * c), :]
        else:
            slope = dz1o[pl.ds((r > 0) * 2 * c, 2 * c), :]
        put_stack(td1, (r + 2) * stack, back * slope)
        own_channels(td1, r + 2, s1, r)

    def third_grad(a):
        total = jnp.zeros((c, 3 * c), F32)
        for r in range(rows // 2):
            mine = tui[pl.ds(pl.multiple_of(r * stack + me * c, c), c), :]
            total = total + dot_t(mine, th2[pl.ds((2 * r + a) * 3 * c, 3 * c), :])
        return total

    def third_grad_use(a, total):
        for b in range(3):
            dw3[pl.ds((a * 3 + b) * c, c), :] = total[:, b * c : (b + 1) * c].astype(BF)

    def kernel_grad(deltas, at):
        total = jnp.zeros((3 * h, 3 * c), F32)
        for q in range(rows + 2):
            ref, base = at(q - 1)
            for par in range(2):
                mine = deltas[par, pl.ds((rows + 1 - q) * h, 3 * h), :]
                total = total + dot_t(mine, ref[pl.ds(base + par * c, 3 * c), :])
        return total

    def kernel_grad_use(out, total):
        for a in range(3):
            for b in range(3):
                out[pl.ds((a * 3 + b) * h, h), :] = total[a * h : (a + 1) * h, b * c : (b + 1) * c].astype(BF)

    def task(does, uses, r):
        return functools.partial(does, r), functools.partial(uses, r)

    z1 = {r: task(first_dot, first_use, r) for r in range(-2, rows + 2)}
    z2 = {r: task(second_dot, second_use, r) for r in range(-1, rows + 1)}
    g2 = {r: task(third_dot, third_use, r) for r in range(-1, rows + 1)}
    g1 = {r: task(back_dot, back_use, r) for r in range(rows)}
    w3 = {a: task(third_grad, third_grad_use, a) for a in range(3)}
    w2 = (lambda: kernel_grad(s2, first_at), functools.partial(kernel_grad_use, dw2))
    w1 = (lambda: kernel_grad(s1, input_at), functools.partial(kernel_grad_use, dw1))
    tasks = [z1[-2], z1[-1], z1[0], z1[rows - 1], z2[-1], z1[rows], z2[0], z1[rows + 1]]
    tasks += [z2[r] for r in range(1, rows)] + [g2[-1], z2[rows]] + [g2[r] for r in range(rows)]
    tasks += [w3[0], g1[0], g2[rows], w3[1]] + [g1[r] for r in range(1, rows - 1)] + [w3[2], g1[rows - 1], w2, w1]

    put_outer(txb, tub, 1 - me, before)
    put_outer(txa, tua, 1 - me, after)
    for out in (s2, s1):
        for par in range(2):
            out[par, pl.ds(0, 2 * h), :] = jnp.zeros((2 * h, m), BF)
            out[par, pl.ds((rows + 2) * h, 2 * h), :] = jnp.zeros((2 * h, m), BF)
    for k in (0, 1, rows + 2, rows + 3):
        td1[pl.ds(k * stack, stack), :] = jnp.zeros((stack, m), BF)
    run(tasks)
    deal((p0, p1, p2, p3), (dw3, dw2, dw1), core[1])


def inputs_kernel(td1, wt1, main, rims):
    h = wt1.shape[0] // 2
    stack = 8 * h
    rows = main.shape[0]
    for k in range(rows + 2):
        back = dot(wt1[...], td1[pl.ds(k * stack, 3 * stack), :])
        flat = jnp.concatenate([back[:h], back[h:]], axis=1)
        if k == 0:
            rims[0] = flat.astype(BF)
        elif k == rows + 1:
            rims[1] = flat.astype(BF)
        else:
            main[k - 1] = flat


def piece_at(tile, k):
    return lax.bitwise_xor(lax.rem(tile, 4), k)


def sum_kernel(*refs):
    total = refs[0][...].astype(F32)
    for piece in refs[1:-1]:
        total = total + piece[...].astype(F32)
    refs[-1][...] = total.astype(BF)


def write_kernel(which, scales, core, *rest):
    pieces, rest = rest[: len(which)], rest[len(which) :]
    outs, held, sems = rest[-5:-2], rest[-2], rest[-1]
    copies = []
    for n, (k, piece) in enumerate(zip(which, pieces)):
        size = piece.shape[0]
        at = piece_at(core[1], k)
        base = 0
        for j, (out, scale) in enumerate(zip(outs, scales)):
            part = out.shape[0] // 4
            here = held.at[pl.ds(n * size + base, part)]
            here[...] = piece[pl.ds(base, part), :].astype(F32) * scale
            there = out.at[pl.ds(pl.multiple_of(at * part, 16), part)]
            copies.append(pltpu.make_async_copy(here, there, sems.at[n, j]))
            copies[-1].start()
            base += part
    for copy in copies:
        copy.wait()


def call(body, name, outs, scratch, limit, *args, aliases=None, far=False):
    vmem = pl.BlockSpec(memory_space=pltpu.VMEM)
    hbm = pl.BlockSpec(memory_space=pl.ANY)
    scalar = pl.BlockSpec(memory_space=pltpu.SMEM)
    return pl.pallas_call(
        body,
        out_shape=tuple(jax.ShapeDtypeStruct(shape, kind) for shape, kind in outs),
        in_specs=[scalar if a.dtype == jnp.int32 else hbm if a.dtype == F32 and far else vmem for a in args],
        out_specs=tuple(hbm if far else vmem for _ in outs),
        scratch_shapes=[pltpu.VMEM(*some) if isinstance(some, tuple) else some for some in scratch],
        compiler_params=pltpu.CompilerParams(vmem_limit_bytes=limit * 1024 * 1024),
        cost_estimate=pl.CostEstimate(flops=10**6, bytes_accessed=10**5, transcendentals=0),
        input_output_aliases=aliases or {},
        name=name,
    )(*args)


def shards(inputs, w_first, w_second, w_third, cotangent, mirror):
    h, rows, cols = inputs.shape
    m = cols // 2
    c = 2 * h
    stack = 4 * c
    tiles = lax.axis_size("blk")
    up = [(i, (i + 1) % tiles) for i in range(tiles)]
    down = [(j, i) for i, j in up]
    core = jnp.stack([lax.axis_index("chan"), lax.axis_index("blk")]).astype(jnp.int32)

    def across(piece):
        return lax.ppermute(piece, "chan", [(0, 1), (1, 0)])

    def swapped(piece, k):
        return lax.ppermute(piece, "blk", [(i, i ^ k) for i in range(tiles)])

    def total(*parts):
        return call(sum_kernel, "sum", [(parts[0].shape, BF)], [], 8, *parts)[0]

    to = lax.broadcasted_iota(jnp.int32, (cols, cols), 1)
    place = 2 * (to % m) + to // m
    place = jnp.where(mirror[0] == 1, cols - 1 - place, place)
    split = (lax.broadcasted_iota(jnp.int32, (cols, cols), 0) == place).astype(BF)
    to = lax.broadcasted_iota(jnp.int32, (m, m), 1)
    place = jnp.where(mirror[0] == 1, m - 1 - to, to)
    turn = (lax.broadcasted_iota(jnp.int32, (m, m), 0) == place).astype(BF)

    x = jnp.einsum("irc,cn->rin", inputs, split, preferred_element_type=F32).astype(BF)
    u = jnp.einsum("orc,cn->ron", cotangent, turn, preferred_element_type=F32).astype(BF)
    u = jnp.concatenate([u[:, :h], u[:, h:]], axis=2)
    before = lax.ppermute(jnp.concatenate([x[rows - 3 :], u[rows // 2 - 1 :]]), "blk", up)
    after = lax.ppermute(jnp.concatenate([x[:3], u[:1]]), "blk", down)
    own = jnp.concatenate([x, u])
    weights, _ = lax.optimization_barrier(([w.reshape(-1, c) for w in (w_first, w_second, w_third)], x))
    weights = [part for w in weights for part in (w, across(w))]
    wb1, wb2, wt2, wt1, wt3e, wt3o, tx, tu, th1, dz1, g2, part1, part2 = call(
        inner_kernel, "inner",
        [
            ((2 * c, 3 * stack), BF),
            ((2 * c, 3 * stack), BF),
            ((2 * c, 3 * stack), BF),
            ((c, 3 * stack), BF),
            ((2 * c, stack), BF),
            ((2 * c, 2 * stack), BF),
            ((rows * stack, m), BF),
            ((rows // 2 * stack, m), BF),
            (((rows - 2) * stack, m), BF),
            (((rows - 2) * 2 * c, m), F32),
            (((rows - 1) * 2 * c, m), F32),
            ((4 * 2 * c, m), F32),
            ((rows * 2 * c, m), F32),
        ],
        [], 24, core, own, across(own), *weights,
    )
    outer = [((3 * stack, m), BF), ((stack, m), BF)]
    before, _ = lax.optimization_barrier((before, g2))
    other_before = across(before)
    txb, tub = call(outer_kernel, "outer", outer, [], 8, core, before)
    after, _ = lax.optimization_barrier((after, txb))
    txa, tua = call(outer_kernel, "outer", outer, [], 8, core, after)

    size = 9 * (c + 2 * h) // 4
    *parts, td1, _, _, _, _ = call(
        main_kernel, "main",
        [((size, c), BF)] * 4 + [(((rows + 4) * stack, m), BF)] + 2 * outer,
        [
            ((6 * stack, m), BF),
            ((2 * 2 * c, m), F32),
            (((rows + 2) * 2 * c, m), F32),
            (((rows + 1) * 3 * c, m), BF),
            (((rows + 2) * stack, m), BF),
            ((2, (rows + 4) * h, m), BF),
            ((2, (rows + 4) * h, m), BF),
            ((9 * h, c), BF),
            ((9 * h, c), BF),
            ((9 * c, c), BF),
        ],
        32, core, txb, tub, txa, tua, other_before, across(after), wb1, wb2, wt2, wt3e, wt3o, tx, tu, th1, dz1, g2, part1, part2,
        aliases={1: 5, 2: 6, 3: 7, 4: 8},
    )
    mine = total(parts[0], *[swapped(part, k) for k, part in enumerate(parts[1:], 1)])
    bit = 4
    while bit < tiles:
        if bit * 2 >= tiles:
            mine, td1 = lax.optimization_barrier((mine, td1))
        mine = total(mine, swapped(mine, bit))
        bit *= 2
    main, rims = call(
        inputs_kernel, "inputs",
        [((rows, h, cols), F32), ((2, h, cols), BF)], [], 16, td1, wt1,
    )
    from_next = lax.ppermute(rims[0], "blk", down)
    from_prev = lax.ppermute(rims[1], "blk", up)
    from_next, _ = lax.optimization_barrier((from_next, mine))
    from_prev, _ = lax.optimization_barrier((from_prev, from_next))
    from_next, from_prev = from_next.astype(F32), from_prev.astype(F32)
    main = jnp.concatenate([main[:1] + from_prev, main[1:-1], main[-1:] + from_next]).astype(BF)
    grad_inputs = jnp.einsum("rin,cn->irc", main, split, preferred_element_type=F32).astype(BF)

    cells = rows * cols * tiles
    wide, narrow = 1.0 / math.sqrt(cells // 4), 1.0 / math.sqrt(cells)
    scales = (wide, narrow, narrow)
    results = [((9 * c, c), F32), ((9 * h, c), F32), ((9 * h, c), F32)]
    far, near = swapped(mine, 3), [swapped(mine, 1), swapped(mine, 2)]
    most = call(
        functools.partial(write_kernel, (0, 1, 2), scales), "most", results,
        [((3 * size, c), F32), pltpu.SemaphoreType.DMA((3, 3))], 8, core, mine, *near, far=True,
    )
    third, second, first = call(
        functools.partial(write_kernel, (3,), scales), "last", results,
        [((size, c), F32), pltpu.SemaphoreType.DMA((1, 3))], 8, core, far, *most, far=True, aliases={2: 0, 3: 1, 4: 2},
    )
    return grad_inputs, first.reshape(3, 3, h, c), second.reshape(3, 3, h, c), third.reshape(3, 3, c, c)


def solution(mesh):
    placed = (
        P("chan", "blk", None),
        P(None, None, "chan", None),
        P(None, None, "chan", None),
        P(None, None, "chan", None),
        P("chan", "blk", None),
        P("blk"),
    )
    return jax.shard_map(
        shards,
        mesh=mesh,
        in_specs=placed,
        out_specs=(
            P("chan", "blk", None),
            P(None, None, "chan", None),
            P(None, None, "chan", None),
            P(None, None, "chan", None),
        ),
        check_vma=False,
    )
```

profile of v0, /device:TPU:0, one launch (start us, length us, event | category | flops | bytes accessed | tf_op | source)
XLA Modules:
  0.0 62.4 jit_solution(2388784335762379311)
XLA Ops:
  0.6 0.0 copy-start
  1.4 0.2 copy-done
  1.7 0.4 fusion
  2.1 0.0 copy-start.3
  2.1 0.5 collective-permute-start.2
  2.6 0.1 collective-permute-start.4
  2.7 0.2 fusion.2
  3.0 0.5 collective-permute-start.1
  3.5 2.6 %collective-permute-start = (bf16[4,64,512]{2,1,0:T(8,128)(2,1)S(1)}, bf16[4,64,512]{2,1,0:T(8,128)(2,1)S(1)}, u32[]{:S(2)}, u32[]{:S(2)}) collective-permute-start(bf16[4,64,512]{2,1,0:T(8,128)(2,1)S(1)} %pad_maximum_fusion.1), channel_id=1, source_target_pairs={{0,2},{2,4},{4,6},{6,8},{8,10},{10,12},{12,14},{14,16},{16,18},{18... | collective-permute-start | bytes 786440 | tf_op jit(solution)/shard_map/ppermute | solution.py:423
  6.2 4.1 %collective-permute-start.5 = (bf16[4,64,512]{2,1,0:T(8,128)(2,1)S(1)}, bf16[4,64,512]{2,1,0:T(8,128)(2,1)S(1)}, u32[]{:S(2)}, u32[]{:S(2)}) collective-permute-start(bf16[4,64,512]{2,1,0:T(8,128)(2,1)S(1)} %fusion.5), channel_id=1, source_target_pairs={{2,0},{4,2},{6,4},{8,6},{10,8},{12,10},{14,12},{16,14},{18,16},{20... | collective-permute-start | bytes 786440 | tf_op jit(solution)/shard_map/ppermute | solution.py:424
  10.2 0.0 collective-permute-done.2.other1
  10.2 0.2 collective-permute-start.3
  10.4 0.1 pad_add_fusion.core
  10.5 1.1 %collective-permute-done.3.other2 = bf16[576,128]{1,0:T(8,128)(2,1)S(1)} collective-permute-done((bf16[576,128]{1,0:T(8,128)(2,1)S(1)}, bf16[576,128]{1,0:T(8,128)(2,1)S(1)}, u32[]{:S(2)}, u32[]{:S(2)}) %collective-permute-start.3) | collective-permute-done | bytes 147488 | tf_op jit(solution)/shard_map/ppermute | solution.py:404
  11.6 0.0 collective-permute-done.4.other3
  11.6 0.0 collective-permute-done.1.other
  11.6 3.0 %inner.1 = (bf16[256,1536]{1,0:T(8,128)(2,1)S(1)}, bf16[256,1536]{1,0:T(8,128)(2,1)S(1)}, bf16[256,1536]{1,0:T(8,128)(2,1)S(1)}, bf16[128,1536]{1,0:T(8,128)(2,1...) custom-call(s32[2]{0:T(128)S(1)} %pad_add_fusion.core, ...), custom_call_target="tpu_custom_call" | custom-call | flops 1000000 | bytes 100000 | tf_op jit(solution)/shard_map/inner/pallas_call | solution.py:380
  14.6 3.3 %collective-permute-done.around = bf16[4,64,512]{2,1,0:T(8,128)(2,1)S(1)} collective-permute-done((bf16[4,64,512]{2,1,0:T(8,128)(2,1)S(1)}, bf16[4,64,512]{2,1,0:T(8,128)(2,1)S(1)}, u32[]{:S(2)}, u32[]{:S(2)}) %collective-permute-start) | collective-permute-done | bytes 262176 | tf_op jit(solution)/shard_map/ppermute | solution.py:423
  17.9 0.7 %outer.2 = (bf16[1536,256]{1,0:T(8,128)(2,1)S(1)}, bf16[512,256]{1,0:T(8,128)(2,1)S(1)}) custom-call(s32[2]{0:T(128)S(1)} %pad_add_fusion.core, bf16[4,64,512]{2,1,0:T(8,128)(2,1)S(1)} %collective-permute-done.around), custom_call_target="tpu_custom_call" | custom-call | flops 1000000 | bytes 100000 | tf_op jit(solution)/shard_map/outer/pallas_call | solution.py:380
  18.6 1.3 %collective-permute-done.5.around = bf16[4,64,512]{2,1,0:T(8,128)(2,1)S(1)} collective-permute-done((bf16[4,64,512]{2,1,0:T(8,128)(2,1)S(1)}, bf16[4,64,512]{2,1,0:T(8,128)(2,1)S(1)}, u32[]{:S(2)}, u32[]{:S(2)}) %collective-permute-start.5) | collective-permute-done | bytes 262176 | tf_op jit(solution)/shard_map/ppermute | solution.py:424
  19.9 0.7 %outer.3 = (bf16[1536,256]{1,0:T(8,128)(2,1)S(1)}, bf16[512,256]{1,0:T(8,128)(2,1)S(1)}) custom-call(s32[2]{0:T(128)S(1)} %pad_add_fusion.core, bf16[4,64,512]{2,1,0:T(8,128)(2,1)S(1)} %collective-permute-done.5.around), custom_call_target="tpu_custom_call" | custom-call | flops 1000000 | bytes 100000 | tf_op jit(solution)/shard_map/outer/pallas_call | solution.py:380
  20.6 0.0 collective-permute-done.6.before
  20.6 0.8 %collective-permute-done.7.after = bf16[4,64,512]{2,1,0:T(8,128)(2,1)S(1)} collective-permute-done((bf16[4,64,512]{2,1,0:T(8,128)(2,1)S(1)}, bf16[4,64,512]{2,1,0:T(8,128)(2,1)S(1)}, u32[]{:S(2)}, u32[]{:S(2)}) %collective-permute-start.7) | collective-permute-done | bytes 262176 | tf_op jit(solution)/shard_map/ppermute | solution.py:404
  21.4 6.9 %main.1 = (bf16[576,128]{1,0:T(8,128)(2,1)S(1)}, bf16[576,128]{1,0:T(8,128)(2,1)S(1)}, bf16[576,128]{1,0:T(8,128)(2,1)S(1)}, bf16[576,128]{1,0:T(8,128)(2,1)S(1)...) custom-call(s32[2]{0:T(128)S(1)} %pad_add_fusion.core, ...), custom_call_target="tpu_custom_call", output_to_operand_aliasing={{5}: (1, {}), {6}: (2, {}), {7}: (3, {}), {8}: (4, {})} | custom-call | flops 1000000 | bytes 100000 | tf_op jit(solution)/shard_map/main/pallas_call | solution.py:380
  28.3 1.6 %collective-permute-start.8 = (bf16[576,128]{1,0:T(8,128)(2,1)S(1)}, bf16[576,128]{1,0:T(8,128)(2,1)S(1)}, u32[]{:S(2)}, u32[]{:S(2)}) collective-permute-start(bf16[576,128]{1,0:T(8,128)(2,1)S(1)} %get-tuple-element.65), channel_id=1, source_target_pairs={{0,2},{2,0},{4,6},{6,4},{8,10},{10,8},{12,14},{14,12},{16,18},{18,... | collective-permute-start | bytes 442376 | tf_op jit(solution)/shard_map/ppermute | solution.py:407
  29.9 0.5 collective-permute-start.9
  30.3 1.5 %collective-permute-start.10 = (bf16[576,128]{1,0:T(8,128)(2,1)S(1)}, bf16[576,128]{1,0:T(8,128)(2,1)S(1)}, u32[]{:S(2)}, u32[]{:S(2)}) collective-permute-start(bf16[576,128]{1,0:T(8,128)(2,1)S(1)} %get-tuple-element.67), channel_id=1, source_target_pairs={{0,6},{2,4},{4,2},{6,0},{8,14},{10,12},{12,10},{14,8},{16,22},{18,... | collective-permute-start | bytes 442376 | tf_op jit(solution)/shard_map/ppermute | solution.py:407
  31.9 2.9 %collective-permute-done.8.refs_1_ = bf16[576,128]{1,0:T(8,128)(2,1)S(1)} collective-permute-done((bf16[576,128]{1,0:T(8,128)(2,1)S(1)}, bf16[576,128]{1,0:T(8,128)(2,1)S(1)}, u32[]{:S(2)}, u32[]{:S(2)}) %collective-permute-start.8) | collective-permute-done | bytes 147488 | tf_op jit(solution)/shard_map/ppermute | solution.py:407
  34.8 2.1 %collective-permute-done.9.refs_2_ = bf16[576,128]{1,0:T(8,128)(2,1)S(1)} collective-permute-done((bf16[576,128]{1,0:T(8,128)(2,1)S(1)}, bf16[576,128]{1,0:T(8,128)(2,1)S(1)}, u32[]{:S(2)}, u32[]{:S(2)}) %collective-permute-start.9) | collective-permute-done | bytes 147488 | tf_op jit(solution)/shard_map/ppermute | solution.py:407
  36.9 1.9 %collective-permute-done.10.refs_3_ = bf16[576,128]{1,0:T(8,128)(2,1)S(1)} collective-permute-done((bf16[576,128]{1,0:T(8,128)(2,1)S(1)}, bf16[576,128]{1,0:T(8,128)(2,1)S(1)}, u32[]{:S(2)}, u32[]{:S(2)}) %collective-permute-start.10) | collective-permute-done | bytes 147488 | tf_op jit(solution)/shard_map/ppermute | solution.py:407
  38.8 0.1 sum.3.refs_0_
  38.9 1.6 %collective-permute-start.11 = (bf16[576,128]{1,0:T(8,128)(2,1)S(1)}, bf16[576,128]{1,0:T(8,128)(2,1)S(1)}, u32[]{:S(2)}, u32[]{:S(2)}) collective-permute-start(bf16[576,128]{1,0:T(8,128)(2,1)S(1)} %sum.3.refs_0_), channel_id=1, source_target_pairs={{0,8},{2,10},{4,12},{6,14},{8,0},{10,2},{12,4},{14,6},{16,24},{18,... | collective-permute-start | bytes 442376 | tf_op jit(solution)/shard_map/ppermute | solution.py:407
  40.6 3.6 %collective-permute-done.11.refs_1_ = bf16[576,128]{1,0:T(8,128)(2,1)S(1)} collective-permute-done((bf16[576,128]{1,0:T(8,128)(2,1)S(1)}, bf16[576,128]{1,0:T(8,128)(2,1)S(1)}, u32[]{:S(2)}, u32[]{:S(2)}) %collective-permute-start.11) | collective-permute-done | bytes 147488 | tf_op jit(solution)/shard_map/ppermute | solution.py:407
  44.2 2.7 %collective-permute-start.14 = (bf16[576,128]{1,0:T(8,128)(2,1)S(1)}, bf16[576,128]{1,0:T(8,128)(2,1)S(1)}, u32[]{:S(2)}, u32[]{:S(2)}) collective-permute-start(bf16[576,128]{1,0:T(8,128)(2,1)S(1)} %sum.4.refs_0_), channel_id=1, source_target_pairs={{0,16},{2,18},{4,20},{6,22},{8,24},{10,26},{12,28},{14,30},{16,0},... | collective-permute-start | bytes 442376 | tf_op jit(solution)/shard_map/ppermute | solution.py:407
  46.8 0.8 %inputs.1 = (f32[4,64,512]{2,1,0:T(8,128)S(1)}, bf16[2,64,512]{2,1,0:T(8,128)(2,1)S(1)}) custom-call(bf16[4096,256]{1,0:T(8,128)(2,1)S(1)} %get-tuple-element.69.td1, bf16[128,1536]{1,0:T(8,128)(2,1)S(1)} %get-tuple-element.70.wt1), custom_call_target="tpu_custom_call" | custom-call | flops 1000000 | bytes 100000 | tf_op jit(solution)/shard_map/inputs/pallas_call | solution.py:380
  47.6 2.1 %collective-permute-start.13 = (bf16[64,512]{1,0:T(8,128)(2,1)S(1)}, bf16[64,512]{1,0:T(8,128)(2,1)S(1)}, u32[]{:S(2)}, u32[]{:S(2)}) collective-permute-start(bf16[64,512]{1,0:T(8,128)(2,1)S(1)} %get-tuple-element.91), channel_id=1, source_target_pairs={{2,0},{4,2},{6,4},{8,6},{10,8},{12,10},{14,12},{16,14},{18,16},{20... | collective-permute-start | bytes 196616 | tf_op jit(solution)/shard_map/ppermute | solution.py:484
  49.8 3.0 %collective-permute-done.14.refs_1_ = bf16[576,128]{1,0:T(8,128)(2,1)S(1)} collective-permute-done((bf16[576,128]{1,0:T(8,128)(2,1)S(1)}, bf16[576,128]{1,0:T(8,128)(2,1)S(1)}, u32[]{:S(2)}, u32[]{:S(2)}) %collective-permute-start.14) | collective-permute-done | bytes 147488 | tf_op jit(solution)/shard_map/ppermute | solution.py:407
  52.8 0.1 collective-permute-start.17
  52.9 1.6 %collective-permute-start.16 = (bf16[576,128]{1,0:T(8,128)(2,1)S(1)}, bf16[576,128]{1,0:T(8,128)(2,1)S(1)}, u32[]{:S(2)}, u32[]{:S(2)}) collective-permute-start(bf16[576,128]{1,0:T(8,128)(2,1)S(1)} %sum.5.rest_0_), channel_id=1, source_target_pairs={{0,2},{2,0},{4,6},{6,4},{8,10},{10,8},{12,14},{14,12},{16,18},{18,... | collective-permute-start | bytes 442376 | tf_op jit(solution)/shard_map/ppermute | solution.py:407
  54.5 1.9 %collective-permute-start.15 = (bf16[576,128]{1,0:T(8,128)(2,1)S(1)}, bf16[576,128]{1,0:T(8,128)(2,1)S(1)}, u32[]{:S(2)}, u32[]{:S(2)}) collective-permute-start(bf16[576,128]{1,0:T(8,128)(2,1)S(1)} %sum.5.rest_0_), channel_id=1, source_target_pairs={{0,6},{2,4},{4,2},{6,0},{8,14},{10,12},{12,10},{14,8},{16,22},{18,... | collective-permute-start | bytes 442376 | tf_op jit(solution)/shard_map/ppermute | solution.py:407
  56.4 0.0 collective-permute-done.13
  56.4 1.4 %collective-permute-done.12 = bf16[64,512]{1,0:T(8,128)(2,1)S(1)} collective-permute-done((bf16[64,512]{1,0:T(8,128)(2,1)S(1)}, bf16[64,512]{1,0:T(8,128)(2,1)S(1)}, u32[]{:S(2)}, u32[]{:S(2)}) %collective-permute-start.12) | collective-permute-done | bytes 65568 | tf_op jit(solution)/shard_map/ppermute | solution.py:485
  57.9 0.4 fusion.1
  58.3 0.9 %copy.19 = bf16[64,4,512]{2,1,0:T(4,128)(2,1)} copy(bf16[64,4,512]{2,0,1:T(8,128)(2,1)S(1)} %fusion.1) | data formatting | bytes 524288
  59.2 0.1 collective-permute-done.17.rest_2_
  59.3 1.5 %most.1 = (f32[1152,128]{1,0:T(8,128)}, f32[576,128]{1,0:T(8,128)}, f32[576,128]{1,0:T(8,128)}) custom-call(s32[2]{0:T(128)S(1)} %pad_add_fusion.core, bf16[576,128]{1,0:T(8,128)(2,1)S(1)} %sum.5.rest_0_, bf16[576,128]{1,0:T(8,128)(2,1)S(1)} %collective-permute-done.16.rest_1_, bf16[576,128]{1,0:T(8,128)(2,1)S(1)} %collective-permute-done.17.rest_2_), custom_call_target="tpu_custom_call" | custom-call | flops 1000000 | bytes 100000 | tf_op jit(solution)/shard_map/most/pallas_call | solution.py:380
  60.8 0.2 collective-permute-done.15.rest_0_
  61.1 1.3 %last.1 = (f32[1152,128]{1,0:T(8,128)}, f32[576,128]{1,0:T(8,128)}, f32[576,128]{1,0:T(8,128)}) custom-call(s32[2]{0:T(128)S(1)} %pad_add_fusion.core, bf16[576,128]{1,0:T(8,128)(2,1)S(1)} %collective-permute-done.15.rest_0_, f32[1152,128]{1,0:T(8,128)} %get-tuple-element.76.rest_1_, ...), custom_call_target="tpu_custom_call", output_to_operand_aliasing={{0}: (2, {}), {1}: (3, {}), {2}: (4, {})} | custom-call | flops 1000000 | bytes 100000 | tf_op jit(solution)/shard_map/last/pallas_call | solution.py:380
  (26 shorter events, 0.3 us)
Async XLA Ops:
  0.6 1.0 %copy-start = (bf16[64,4,512]{2,1,0:T(4,128)(2,1)S(1)}, bf16[64,4,512]{2,1,0:T(4,128)(2,1)}, u32[]{:S(2)}) copy-start(bf16[64,4,512]{2,1,0:T(4,128)(2,1)} %param.6) | copy-start | bytes 786436
  0.6 2.0 %copy-start.1 = (bf16[3,3,128,128]{3,2,1,0:T(8,128)(2,1)S(1)}, bf16[3,3,128,128]{3,2,1,0:T(8,128)(2,1)}, u32[]{:S(2)}) copy-start(bf16[3,3,128,128]{3,2,1,0:T(8,128)(2,1)} %param.9) | copy-start | bytes 884740
  0.7 1.4 %copy-start.2 = (bf16[3,3,64,128]{3,2,1,0:T(8,128)(2,1)S(1)}, bf16[3,3,64,128]{3,2,1,0:T(8,128)(2,1)}, u32[]{:S(2)}) copy-start(bf16[3,3,64,128]{3,2,1,0:T(8,128)(2,1)} %param.7) | copy-start | bytes 442372
  0.7 2.0 %copy-start.4 = (bf16[128,2,256]{2,1,0:T(2,128)(2,1)S(1)}, bf16[128,2,256]{2,1,0:T(2,128)(2,1)}, u32[]{:S(2)}) copy-start(bf16[128,2,256]{2,1,0:T(2,128)(2,1)} %param.10) | copy-start | bytes 393220
  2.1 8.2 %copy-start.3 = (bf16[3,3,64,128]{3,2,1,0:T(8,128)(2,1)S(1)}, bf16[3,3,64,128]{3,2,1,0:T(8,128)(2,1)}, u32[]{:S(2)}) copy-start(bf16[3,3,64,128]{3,2,1,0:T(8,128)(2,1)} %param.8) | copy-start | bytes 442372
  2.1 8.2 %collective-permute-start.2 = (bf16[576,128]{1,0:T(8,128)(2,1)S(1)}, bf16[576,128]{1,0:T(8,128)(2,1)S(1)}, u32[]{:S(2)}, u32[]{:S(2)}) collective-permute-start(bf16[576,128]{1,0:T(8,128)(2,1)S(1)} %bitcast.34), channel_id=1, source_target_pairs={{0,1},{1,0},{2,3},{3,2},{4,5},{5,4},{6,7},{7,6},{8,9},{9,8},{10,11... | collective-permute-start | bytes 442376 | tf_op jit(solution)/shard_map/ppermute | solution.py:404
  2.6 9.0 %collective-permute-start.4 = (bf16[1152,128]{1,0:T(8,128)(2,1)S(1)}, bf16[1152,128]{1,0:T(8,128)(2,1)S(1)}, u32[]{:S(2)}, u32[]{:S(2)}) collective-permute-start(bf16[1152,128]{1,0:T(8,128)(2,1)S(1)} %bitcast.32), channel_id=1, source_target_pairs={{0,1},{1,0},{2,3},{3,2},{4,5},{5,4},{6,7},{7,6},{8,9},{9,8},{10,11... | collective-permute-start | bytes 884744 | tf_op jit(solution)/shard_map/ppermute | solution.py:404
  3.0 8.7 %collective-permute-start.1 = (bf16[6,64,512]{2,1,0:T(8,128)(2,1)S(1)}, bf16[6,64,512]{2,1,0:T(8,128)(2,1)S(1)}, u32[]{:S(2)}, u32[]{:S(2)}) collective-permute-start(bf16[6,64,512]{2,1,0:T(8,128)(2,1)S(1)} %maximum_maximum_fusion.own), channel_id=1, source_target_pairs={{0,1},{1,0},{2,3},{3,2},{4,5},{5,4},{6,7},{7,6},{8,9},{9,8},{10,11... | collective-permute-start | bytes 1179656 | tf_op jit(solution)/shard_map/ppermute | solution.py:404
  3.5 14.4 %collective-permute-start = (bf16[4,64,512]{2,1,0:T(8,128)(2,1)S(1)}, bf16[4,64,512]{2,1,0:T(8,128)(2,1)S(1)}, u32[]{:S(2)}, u32[]{:S(2)}) collective-permute-start(bf16[4,64,512]{2,1,0:T(8,128)(2,1)S(1)} %pad_maximum_fusion.1), channel_id=1, source_target_pairs={{0,2},{2,4},{4,6},{6,8},{8,10},{10,12},{12,14},{14,16},{16,18},{18... | collective-permute-start | bytes 786440 | tf_op jit(solution)/shard_map/ppermute | solution.py:423
  6.2 13.7 %collective-permute-start.5 = (bf16[4,64,512]{2,1,0:T(8,128)(2,1)S(1)}, bf16[4,64,512]{2,1,0:T(8,128)(2,1)S(1)}, u32[]{:S(2)}, u32[]{:S(2)}) collective-permute-start(bf16[4,64,512]{2,1,0:T(8,128)(2,1)S(1)} %fusion.5), channel_id=1, source_target_pairs={{2,0},{4,2},{6,4},{8,6},{10,8},{12,10},{14,12},{16,14},{18,16},{20... | collective-permute-start | bytes 786440 | tf_op jit(solution)/shard_map/ppermute | solution.py:424
  10.2 1.4 %collective-permute-start.3 = (bf16[576,128]{1,0:T(8,128)(2,1)S(1)}, bf16[576,128]{1,0:T(8,128)(2,1)S(1)}, u32[]{:S(2)}, u32[]{:S(2)}) collective-permute-start(bf16[576,128]{1,0:T(8,128)(2,1)S(1)} %bitcast.36), channel_id=1, source_target_pairs={{0,1},{1,0},{2,3},{3,2},{4,5},{5,4},{6,7},{7,6},{8,9},{9,8},{10,11... | collective-permute-start | bytes 442376 | tf_op jit(solution)/shard_map/ppermute | solution.py:404
  17.9 2.6 %collective-permute-start.6 = (bf16[4,64,512]{2,1,0:T(8,128)(2,1)S(1)}, bf16[4,64,512]{2,1,0:T(8,128)(2,1)S(1)}, u32[]{:S(2)}, u32[]{:S(2)}) collective-permute-start(bf16[4,64,512]{2,1,0:T(8,128)(2,1)S(1)} %collective-permute-done.around), channel_id=1, source_target_pairs={{0,1},{1,0},{2,3},{3,2},{4,5},{5,4},{6,7},{7,6},{8,9},{9,8},{10,11... | collective-permute-start | bytes 786440 | tf_op jit(solution)/shard_map/ppermute | solution.py:404
  19.9 1.5 %collective-permute-start.7 = (bf16[4,64,512]{2,1,0:T(8,128)(2,1)S(1)}, bf16[4,64,512]{2,1,0:T(8,128)(2,1)S(1)}, u32[]{:S(2)}, u32[]{:S(2)}) collective-permute-start(bf16[4,64,512]{2,1,0:T(8,128)(2,1)S(1)} %collective-permute-done.5.around), channel_id=1, source_target_pairs={{0,1},{1,0},{2,3},{3,2},{4,5},{5,4},{6,7},{7,6},{8,9},{9,8},{10,11... | collective-permute-start | bytes 786440 | tf_op jit(solution)/shard_map/ppermute | solution.py:404
  28.3 6.5 %collective-permute-start.8 = (bf16[576,128]{1,0:T(8,128)(2,1)S(1)}, bf16[576,128]{1,0:T(8,128)(2,1)S(1)}, u32[]{:S(2)}, u32[]{:S(2)}) collective-permute-start(bf16[576,128]{1,0:T(8,128)(2,1)S(1)} %get-tuple-element.65), channel_id=1, source_target_pairs={{0,2},{2,0},{4,6},{6,4},{8,10},{10,8},{12,14},{14,12},{16,18},{18,... | collective-permute-start | bytes 442376 | tf_op jit(solution)/shard_map/ppermute | solution.py:407
  29.9 7.0 %collective-permute-start.9 = (bf16[576,128]{1,0:T(8,128)(2,1)S(1)}, bf16[576,128]{1,0:T(8,128)(2,1)S(1)}, u32[]{:S(2)}, u32[]{:S(2)}) collective-permute-start(bf16[576,128]{1,0:T(8,128)(2,1)S(1)} %get-tuple-element.66), channel_id=1, source_target_pairs={{0,4},{2,6},{4,0},{6,2},{8,12},{10,14},{12,8},{14,10},{16,20},{18,... | collective-permute-start | bytes 442376 | tf_op jit(solution)/shard_map/ppermute | solution.py:407
  30.3 8.5 %collective-permute-start.10 = (bf16[576,128]{1,0:T(8,128)(2,1)S(1)}, bf16[576,128]{1,0:T(8,128)(2,1)S(1)}, u32[]{:S(2)}, u32[]{:S(2)}) collective-permute-start(bf16[576,128]{1,0:T(8,128)(2,1)S(1)} %get-tuple-element.67), channel_id=1, source_target_pairs={{0,6},{2,4},{4,2},{6,0},{8,14},{10,12},{12,10},{14,8},{16,22},{18,... | collective-permute-start | bytes 442376 | tf_op jit(solution)/shard_map/ppermute | solution.py:407
  38.9 5.2 %collective-permute-start.11 = (bf16[576,128]{1,0:T(8,128)(2,1)S(1)}, bf16[576,128]{1,0:T(8,128)(2,1)S(1)}, u32[]{:S(2)}, u32[]{:S(2)}) collective-permute-start(bf16[576,128]{1,0:T(8,128)(2,1)S(1)} %sum.3.refs_0_), channel_id=1, source_target_pairs={{0,8},{2,10},{4,12},{6,14},{8,0},{10,2},{12,4},{14,6},{16,24},{18,... | collective-permute-start | bytes 442376 | tf_op jit(solution)/shard_map/ppermute | solution.py:407
  44.2 8.6 %collective-permute-start.14 = (bf16[576,128]{1,0:T(8,128)(2,1)S(1)}, bf16[576,128]{1,0:T(8,128)(2,1)S(1)}, u32[]{:S(2)}, u32[]{:S(2)}) collective-permute-start(bf16[576,128]{1,0:T(8,128)(2,1)S(1)} %sum.4.refs_0_), channel_id=1, source_target_pairs={{0,16},{2,18},{4,20},{6,22},{8,24},{10,26},{12,28},{14,30},{16,0},... | collective-permute-start | bytes 442376 | tf_op jit(solution)/shard_map/ppermute | solution.py:407
  47.6 8.8 %collective-permute-start.13 = (bf16[64,512]{1,0:T(8,128)(2,1)S(1)}, bf16[64,512]{1,0:T(8,128)(2,1)S(1)}, u32[]{:S(2)}, u32[]{:S(2)}) collective-permute-start(bf16[64,512]{1,0:T(8,128)(2,1)S(1)} %get-tuple-element.91), channel_id=1, source_target_pairs={{2,0},{4,2},{6,4},{8,6},{10,8},{12,10},{14,12},{16,14},{18,16},{20... | collective-permute-start | bytes 196616 | tf_op jit(solution)/shard_map/ppermute | solution.py:484
  49.8 8.1 %collective-permute-start.12 = (bf16[64,512]{1,0:T(8,128)(2,1)S(1)}, bf16[64,512]{1,0:T(8,128)(2,1)S(1)}, u32[]{:S(2)}, u32[]{:S(2)}) collective-permute-start(bf16[64,512]{1,0:T(8,128)(2,1)S(1)} %get-tuple-element.90), channel_id=1, source_target_pairs={{0,2},{2,4},{4,6},{6,8},{8,10},{10,12},{12,14},{14,16},{16,18},{18... | collective-permute-start | bytes 196616 | tf_op jit(solution)/shard_map/ppermute | solution.py:485
  52.8 6.5 %collective-permute-start.17 = (bf16[576,128]{1,0:T(8,128)(2,1)S(1)}, bf16[576,128]{1,0:T(8,128)(2,1)S(1)}, u32[]{:S(2)}, u32[]{:S(2)}) collective-permute-start(bf16[576,128]{1,0:T(8,128)(2,1)S(1)} %sum.5.rest_0_), channel_id=1, source_target_pairs={{0,4},{2,6},{4,0},{6,2},{8,12},{10,14},{12,8},{14,10},{16,20},{18,... | collective-permute-start | bytes 442376 | tf_op jit(solution)/shard_map/ppermute | solution.py:407
  52.9 6.4 %collective-permute-start.16 = (bf16[576,128]{1,0:T(8,128)(2,1)S(1)}, bf16[576,128]{1,0:T(8,128)(2,1)S(1)}, u32[]{:S(2)}, u32[]{:S(2)}) collective-permute-start(bf16[576,128]{1,0:T(8,128)(2,1)S(1)} %sum.5.rest_0_), channel_id=1, source_target_pairs={{0,2},{2,0},{4,6},{6,4},{8,10},{10,8},{12,14},{14,12},{16,18},{18,... | collective-permute-start | bytes 442376 | tf_op jit(solution)/shard_map/ppermute | solution.py:407
  54.5 6.6 %collective-permute-start.15 = (bf16[576,128]{1,0:T(8,128)(2,1)S(1)}, bf16[576,128]{1,0:T(8,128)(2,1)S(1)}, u32[]{:S(2)}, u32[]{:S(2)}) collective-permute-start(bf16[576,128]{1,0:T(8,128)(2,1)S(1)} %sum.5.rest_0_), channel_id=1, source_target_pairs={{0,6},{2,4},{4,2},{6,0},{8,14},{10,12},{12,10},{14,8},{16,22},{18,... | collective-permute-start | bytes 442376 | tf_op jit(solution)/shard_map/ppermute | solution.py:407
where the time goes:
time: 62.5 us; the launch traced here: 62.4 us
  waiting for transfers between devices  21.9 us (35%)
  starting transfers between devices  21.5 us (34%)
  Pallas kernels  15 us (24%)
  between operations  1.58 us (3%)
  local copies, waits for them, and re-layouts  1.24 us (2%)
  matrix products  0.98 us (2%)
    pallas_call x10, Pallas kernels, call(): pl.pallas_call(body, out_shape=tuple((jax.ShapeDtypeStruct(shape, kind) f...  15 us
    ppermute x8, waiting for transfers between devices, swapped(): return lax.ppermute(piece, 'blk', [(i, i ^ k) for i in range(tiles)])  13.9 us
    ppermute x8, starting transfers between devices, swapped(): return lax.ppermute(piece, 'blk', [(i, i ^ k) for i in range(tiles)])  11.4 us
    ppermute x1, starting transfers between devices, shards(): after = lax.ppermute(jnp.concatenate([x[:3], u[:1]]), 'blk', down)  4.06 us
    ppermute x1, waiting for transfers between devices, shards(): lax.ppermute(jnp.concatenate([x[rows - 3:], u[rows // 2 - 1:]]), 'blk', up)  3.32 us
    ppermute x1, starting transfers between devices, shards(): lax.ppermute(jnp.concatenate([x[rows - 3:], u[rows // 2 - 1:]]), 'blk', up)  2.63 us
    ppermute x1, starting transfers between devices, shards(): from_next = lax.ppermute(rims[0], 'blk', down)  2.13 us
    ppermute x6, waiting for transfers between devices, across(): return lax.ppermute(piece, 'chan', [(0, 1), (1, 0)])  1.98 us
  transfers between devices with their start and end apart: 18, of which 12 were waited for; matrix products, arithmetic and copies ran while one was open for 3% of the time, Pallas kernels for 11%

commit v1 on v0

--- a/solution.py
+++ b/solution.py
@@ -277,24 +277,24 @@
         own_channels(td1, r + 2, s1, r)
 
     def third_grad(a):
-        total = jnp.zeros((c, 3 * c), F32)
+        left, right = [], []
         for r in range(rows // 2):
-            mine = tui[pl.ds(pl.multiple_of(r * stack + me * c, c), c), :]
-            total = total + dot_t(mine, th2[pl.ds((2 * r + a) * 3 * c, 3 * c), :])
-        return total
+            left.append(tui[pl.ds(pl.multiple_of(r * stack + me * c, c), c), :])
+            right.append(th2[pl.ds((2 * r + a) * 3 * c, 3 * c), :])
+        return dot_t(jnp.concatenate(left, axis=1), jnp.concatenate(right, axis=1))
 
     def third_grad_use(a, total):
         for b in range(3):
             dw3[pl.ds((a * 3 + b) * c, c), :] = total[:, b * c : (b + 1) * c].astype(BF)
 
     def kernel_grad(deltas, at):
-        total = jnp.zeros((3 * h, 3 * c), F32)
+        left, right = [], []
         for q in range(rows + 2):
             ref, base = at(q - 1)
             for par in range(2):
-                mine = deltas[par, pl.ds((rows + 1 - q) * h, 3 * h), :]
-                total = total + dot_t(mine, ref[pl.ds(base + par * c, 3 * c), :])
-        return total
+                left.append(deltas[par, pl.ds((rows + 1 - q) * h, 3 * h), :])
+                right.append(ref[pl.ds(base + par * c, 3 * c), :])
+        return dot_t(jnp.concatenate(left, axis=1), jnp.concatenate(right, axis=1))
 
     def kernel_grad_use(out, total):
         for a in range(3):

time: 62.5 us -> 62.4 us (level)
  no operation moved by 1% of the time
where the time goes in v1:
time: 62.4 us; the launch traced here: 62.3 us
  waiting for transfers between devices  21.9 us (35%)
  starting transfers between devices  21.5 us (34%)
  Pallas kernels  14.9 us (24%)
  between operations  1.58 us (3%)
  local copies, waits for them, and re-layouts  1.24 us (2%)
  matrix products  0.98 us (2%)
    pallas_call x10, Pallas kernels, call(): pl.pallas_call(body, out_shape=tuple((jax.ShapeDtypeStruct(shape, kind) f...  14.9 us
    ppermute x8, waiting for transfers between devices, swapped(): return lax.ppermute(piece, 'blk', [(i, i ^ k) for i in range(tiles)])  14 us
    ppermute x8, starting transfers between devices, swapped(): return lax.ppermute(piece, 'blk', [(i, i ^ k) for i in range(tiles)])  11.4 us
    ppermute x1, starting transfers between devices, shards(): after = lax.ppermute(jnp.concatenate([x[:3], u[:1]]), 'blk', down)  4.06 us
    ppermute x1, waiting for transfers between devices, shards(): lax.ppermute(jnp.concatenate([x[rows - 3:], u[rows // 2 - 1:]]), 'blk', up)  3.32 us
    ppermute x1, starting transfers between devices, shards(): lax.ppermute(jnp.concatenate([x[rows - 3:], u[rows // 2 - 1:]]), 'blk', up)  2.63 us
    ppermute x1, starting transfers between devices, shards(): from_next = lax.ppermute(rims[0], 'blk', down)  2.13 us
    ppermute x6, waiting for transfers between devices, across(): return lax.ppermute(piece, 'chan', [(0, 1), (1, 0)])  1.98 us
  transfers between devices with their start and end apart: 18, of which 12 were waited for; matrix products, arithmetic and copies ran while one was open for 3% of the time, Pallas kernels for 11%

profile of v1, /device:TPU:0, one launch (start us, length us, event | category | flops | bytes accessed | tf_op | source)
XLA Modules:
  0.0 62.3 jit_solution(17619429725634732569)
XLA Ops:
  0.6 0.0 copy-start
  1.4 0.2 copy-done
  1.7 0.4 fusion
  2.1 0.0 copy-start.3
  2.1 0.5 collective-permute-start.2
  2.6 0.1 collective-permute-start.4
  2.7 0.2 fusion.2
  3.0 0.5 collective-permute-start.1
  3.5 2.6 %collective-permute-start = (bf16[4,64,512]{2,1,0:T(8,128)(2,1)S(1)}, bf16[4,64,512]{2,1,0:T(8,128)(2,1)S(1)}, u32[]{:S(2)}, u32[]{:S(2)}) collective-permute-start(bf16[4,64,512]{2,1,0:T(8,128)(2,1)S(1)} %pad_maximum_fusion.1), channel_id=1, source_target_pairs={{0,2},{2,4},{4,6},{6,8},{8,10},{10,12},{12,14},{14,16},{16,18},{18... | collective-permute-start | bytes 786440 | tf_op jit(solution)/shard_map/ppermute | solution.py:423
  6.2 4.1 %collective-permute-start.5 = (bf16[4,64,512]{2,1,0:T(8,128)(2,1)S(1)}, bf16[4,64,512]{2,1,0:T(8,128)(2,1)S(1)}, u32[]{:S(2)}, u32[]{:S(2)}) collective-permute-start(bf16[4,64,512]{2,1,0:T(8,128)(2,1)S(1)} %fusion.5), channel_id=1, source_target_pairs={{2,0},{4,2},{6,4},{8,6},{10,8},{12,10},{14,12},{16,14},{18,16},{20... | collective-permute-start | bytes 786440 | tf_op jit(solution)/shard_map/ppermute | solution.py:424
  10.2 0.0 collective-permute-done.2.other1
  10.2 0.2 collective-permute-start.3
  10.4 0.1 pad_add_fusion.core
  10.5 1.1 %collective-permute-done.3.other2 = bf16[576,128]{1,0:T(8,128)(2,1)S(1)} collective-permute-done((bf16[576,128]{1,0:T(8,128)(2,1)S(1)}, bf16[576,128]{1,0:T(8,128)(2,1)S(1)}, u32[]{:S(2)}, u32[]{:S(2)}) %collective-permute-start.3) | collective-permute-done | bytes 147488 | tf_op jit(solution)/shard_map/ppermute | solution.py:404
  11.6 0.0 collective-permute-done.4.other3
  11.6 0.0 collective-permute-done.1.other
  11.6 3.0 %inner.1 = (bf16[256,1536]{1,0:T(8,128)(2,1)S(1)}, bf16[256,1536]{1,0:T(8,128)(2,1)S(1)}, bf16[256,1536]{1,0:T(8,128)(2,1)S(1)}, bf16[128,1536]{1,0:T(8,128)(2,1...) custom-call(s32[2]{0:T(128)S(1)} %pad_add_fusion.core, ...), custom_call_target="tpu_custom_call" | custom-call | flops 1000000 | bytes 100000 | tf_op jit(solution)/shard_map/inner/pallas_call | solution.py:380
  14.6 3.3 %collective-permute-done.around = bf16[4,64,512]{2,1,0:T(8,128)(2,1)S(1)} collective-permute-done((bf16[4,64,512]{2,1,0:T(8,128)(2,1)S(1)}, bf16[4,64,512]{2,1,0:T(8,128)(2,1)S(1)}, u32[]{:S(2)}, u32[]{:S(2)}) %collective-permute-start) | collective-permute-done | bytes 262176 | tf_op jit(solution)/shard_map/ppermute | solution.py:423
  17.9 0.0 collective-permute-start.6
  17.9 0.7 %outer.2 = (bf16[1536,256]{1,0:T(8,128)(2,1)S(1)}, bf16[512,256]{1,0:T(8,128)(2,1)S(1)}) custom-call(s32[2]{0:T(128)S(1)} %pad_add_fusion.core, bf16[4,64,512]{2,1,0:T(8,128)(2,1)S(1)} %collective-permute-done.around), custom_call_target="tpu_custom_call" | custom-call | flops 1000000 | bytes 100000 | tf_op jit(solution)/shard_map/outer/pallas_call | solution.py:380
  18.6 1.3 %collective-permute-done.5.around = bf16[4,64,512]{2,1,0:T(8,128)(2,1)S(1)} collective-permute-done((bf16[4,64,512]{2,1,0:T(8,128)(2,1)S(1)}, bf16[4,64,512]{2,1,0:T(8,128)(2,1)S(1)}, u32[]{:S(2)}, u32[]{:S(2)}) %collective-permute-start.5) | collective-permute-done | bytes 262176 | tf_op jit(solution)/shard_map/ppermute | solution.py:424
  19.9 0.0 collective-permute-start.7
  19.9 0.7 %outer.3 = (bf16[1536,256]{1,0:T(8,128)(2,1)S(1)}, bf16[512,256]{1,0:T(8,128)(2,1)S(1)}) custom-call(s32[2]{0:T(128)S(1)} %pad_add_fusion.core, bf16[4,64,512]{2,1,0:T(8,128)(2,1)S(1)} %collective-permute-done.5.around), custom_call_target="tpu_custom_call" | custom-call | flops 1000000 | bytes 100000 | tf_op jit(solution)/shard_map/outer/pallas_call | solution.py:380
  20.6 0.8 %collective-permute-done.7.after = bf16[4,64,512]{2,1,0:T(8,128)(2,1)S(1)} collective-permute-done((bf16[4,64,512]{2,1,0:T(8,128)(2,1)S(1)}, bf16[4,64,512]{2,1,0:T(8,128)(2,1)S(1)}, u32[]{:S(2)}, u32[]{:S(2)}) %collective-permute-start.7) | collective-permute-done | bytes 262176 | tf_op jit(solution)/shard_map/ppermute | solution.py:404
  21.4 6.8 %main.1 = (bf16[576,128]{1,0:T(8,128)(2,1)S(1)}, bf16[576,128]{1,0:T(8,128)(2,1)S(1)}, bf16[576,128]{1,0:T(8,128)(2,1)S(1)}, bf16[576,128]{1,0:T(8,128)(2,1)S(1)...) custom-call(s32[2]{0:T(128)S(1)} %pad_add_fusion.core, ...), custom_call_target="tpu_custom_call", output_to_operand_aliasing={{5}: (1, {}), {6}: (2, {}), {7}: (3, {}), {8}: (4, {})} | custom-call | flops 1000000 | bytes 100000 | tf_op jit(solution)/shard_map/main/pallas_call | solution.py:380
  28.2 1.6 %collective-permute-start.8 = (bf16[576,128]{1,0:T(8,128)(2,1)S(1)}, bf16[576,128]{1,0:T(8,128)(2,1)S(1)}, u32[]{:S(2)}, u32[]{:S(2)}) collective-permute-start(bf16[576,128]{1,0:T(8,128)(2,1)S(1)} %get-tuple-element.65), channel_id=1, source_target_pairs={{0,2},{2,0},{4,6},{6,4},{8,10},{10,8},{12,14},{14,12},{16,18},{18,... | collective-permute-start | bytes 442376 | tf_op jit(solution)/shard_map/ppermute | solution.py:407
  29.8 0.4 collective-permute-start.9
  30.2 1.6 %collective-permute-start.10 = (bf16[576,128]{1,0:T(8,128)(2,1)S(1)}, bf16[576,128]{1,0:T(8,128)(2,1)S(1)}, u32[]{:S(2)}, u32[]{:S(2)}) collective-permute-start(bf16[576,128]{1,0:T(8,128)(2,1)S(1)} %get-tuple-element.67), channel_id=1, source_target_pairs={{0,6},{2,4},{4,2},{6,0},{8,14},{10,12},{12,10},{14,8},{16,22},{18,... | collective-permute-start | bytes 442376 | tf_op jit(solution)/shard_map/ppermute | solution.py:407
  31.7 2.9 %collective-permute-done.8.refs_1_ = bf16[576,128]{1,0:T(8,128)(2,1)S(1)} collective-permute-done((bf16[576,128]{1,0:T(8,128)(2,1)S(1)}, bf16[576,128]{1,0:T(8,128)(2,1)S(1)}, u32[]{:S(2)}, u32[]{:S(2)}) %collective-permute-start.8) | collective-permute-done | bytes 147488 | tf_op jit(solution)/shard_map/ppermute | solution.py:407
  34.7 2.1 %collective-permute-done.9.refs_2_ = bf16[576,128]{1,0:T(8,128)(2,1)S(1)} collective-permute-done((bf16[576,128]{1,0:T(8,128)(2,1)S(1)}, bf16[576,128]{1,0:T(8,128)(2,1)S(1)}, u32[]{:S(2)}, u32[]{:S(2)}) %collective-permute-start.9) | collective-permute-done | bytes 147488 | tf_op jit(solution)/shard_map/ppermute | solution.py:407
  36.8 1.9 %collective-permute-done.10.refs_3_ = bf16[576,128]{1,0:T(8,128)(2,1)S(1)} collective-permute-done((bf16[576,128]{1,0:T(8,128)(2,1)S(1)}, bf16[576,128]{1,0:T(8,128)(2,1)S(1)}, u32[]{:S(2)}, u32[]{:S(2)}) %collective-permute-start.10) | collective-permute-done | bytes 147488 | tf_op jit(solution)/shard_map/ppermute | solution.py:407
  38.7 0.1 sum.3.refs_0_
  38.8 1.6 %collective-permute-start.11 = (bf16[576,128]{1,0:T(8,128)(2,1)S(1)}, bf16[576,128]{1,0:T(8,128)(2,1)S(1)}, u32[]{:S(2)}, u32[]{:S(2)}) collective-permute-start(bf16[576,128]{1,0:T(8,128)(2,1)S(1)} %sum.3.refs_0_), channel_id=1, source_target_pairs={{0,8},{2,10},{4,12},{6,14},{8,0},{10,2},{12,4},{14,6},{16,24},{18,... | collective-permute-start | bytes 442376 | tf_op jit(solution)/shard_map/ppermute | solution.py:407
  40.4 3.6 %collective-permute-done.11.refs_1_ = bf16[576,128]{1,0:T(8,128)(2,1)S(1)} collective-permute-done((bf16[576,128]{1,0:T(8,128)(2,1)S(1)}, bf16[576,128]{1,0:T(8,128)(2,1)S(1)}, u32[]{:S(2)}, u32[]{:S(2)}) %collective-permute-start.11) | collective-permute-done | bytes 147488 | tf_op jit(solution)/shard_map/ppermute | solution.py:407
  44.0 2.7 %collective-permute-start.14 = (bf16[576,128]{1,0:T(8,128)(2,1)S(1)}, bf16[576,128]{1,0:T(8,128)(2,1)S(1)}, u32[]{:S(2)}, u32[]{:S(2)}) collective-permute-start(bf16[576,128]{1,0:T(8,128)(2,1)S(1)} %sum.4.refs_0_), channel_id=1, source_target_pairs={{0,16},{2,18},{4,20},{6,22},{8,24},{10,26},{12,28},{14,30},{16,0},... | collective-permute-start | bytes 442376 | tf_op jit(solution)/shard_map/ppermute | solution.py:407
  46.7 0.8 %inputs.1 = (f32[4,64,512]{2,1,0:T(8,128)S(1)}, bf16[2,64,512]{2,1,0:T(8,128)(2,1)S(1)}) custom-call(bf16[4096,256]{1,0:T(8,128)(2,1)S(1)} %get-tuple-element.69.td1, bf16[128,1536]{1,0:T(8,128)(2,1)S(1)} %get-tuple-element.70.wt1), custom_call_target="tpu_custom_call" | custom-call | flops 1000000 | bytes 100000 | tf_op jit(solution)/shard_map/inputs/pallas_call | solution.py:380
  47.5 2.1 %collective-permute-start.13 = (bf16[64,512]{1,0:T(8,128)(2,1)S(1)}, bf16[64,512]{1,0:T(8,128)(2,1)S(1)}, u32[]{:S(2)}, u32[]{:S(2)}) collective-permute-start(bf16[64,512]{1,0:T(8,128)(2,1)S(1)} %get-tuple-element.91), channel_id=1, source_target_pairs={{2,0},{4,2},{6,4},{8,6},{10,8},{12,10},{14,12},{16,14},{18,16},{20... | collective-permute-start | bytes 196616 | tf_op jit(solution)/shard_map/ppermute | solution.py:484
  49.6 3.0 %collective-permute-done.14.refs_1_ = bf16[576,128]{1,0:T(8,128)(2,1)S(1)} collective-permute-done((bf16[576,128]{1,0:T(8,128)(2,1)S(1)}, bf16[576,128]{1,0:T(8,128)(2,1)S(1)}, u32[]{:S(2)}, u32[]{:S(2)}) %collective-permute-start.14) | collective-permute-done | bytes 147488 | tf_op jit(solution)/shard_map/ppermute | solution.py:407
  52.7 0.1 collective-permute-start.17
  52.8 1.6 %collective-permute-start.16 = (bf16[576,128]{1,0:T(8,128)(2,1)S(1)}, bf16[576,128]{1,0:T(8,128)(2,1)S(1)}, u32[]{:S(2)}, u32[]{:S(2)}) collective-permute-start(bf16[576,128]{1,0:T(8,128)(2,1)S(1)} %sum.5.rest_0_), channel_id=1, source_target_pairs={{0,2},{2,0},{4,6},{6,4},{8,10},{10,8},{12,14},{14,12},{16,18},{18,... | collective-permute-start | bytes 442376 | tf_op jit(solution)/shard_map/ppermute | solution.py:407
  54.4 1.9 %collective-permute-start.15 = (bf16[576,128]{1,0:T(8,128)(2,1)S(1)}, bf16[576,128]{1,0:T(8,128)(2,1)S(1)}, u32[]{:S(2)}, u32[]{:S(2)}) collective-permute-start(bf16[576,128]{1,0:T(8,128)(2,1)S(1)} %sum.5.rest_0_), channel_id=1, source_target_pairs={{0,6},{2,4},{4,2},{6,0},{8,14},{10,12},{12,10},{14,8},{16,22},{18,... | collective-permute-start | bytes 442376 | tf_op jit(solution)/shard_map/ppermute | solution.py:407
  56.3 1.4 %collective-permute-done.12 = bf16[64,512]{1,0:T(8,128)(2,1)S(1)} collective-permute-done((bf16[64,512]{1,0:T(8,128)(2,1)S(1)}, bf16[64,512]{1,0:T(8,128)(2,1)S(1)}, u32[]{:S(2)}, u32[]{:S(2)}) %collective-permute-start.12) | collective-permute-done | bytes 65568 | tf_op jit(solution)/shard_map/ppermute | solution.py:485
  57.7 0.4 fusion.1
  58.1 0.9 %copy.19 = bf16[64,4,512]{2,1,0:T(4,128)(2,1)} copy(bf16[64,4,512]{2,0,1:T(8,128)(2,1)S(1)} %fusion.1) | data formatting | bytes 524288
  59.0 0.2 collective-permute-done.17.rest_2_
  59.2 1.5 %most.1 = (f32[1152,128]{1,0:T(8,128)}, f32[576,128]{1,0:T(8,128)}, f32[576,128]{1,0:T(8,128)}) custom-call(s32[2]{0:T(128)S(1)} %pad_add_fusion.core, bf16[576,128]{1,0:T(8,128)(2,1)S(1)} %sum.5.rest_0_, bf16[576,128]{1,0:T(8,128)(2,1)S(1)} %collective-permute-done.16.rest_1_, bf16[576,128]{1,0:T(8,128)(2,1)S(1)} %collective-permute-done.17.rest_2_), custom_call_target="tpu_custom_call" | custom-call | flops 1000000 | bytes 100000 | tf_op jit(solution)/shard_map/most/pallas_call | solution.py:380
  60.8 0.2 collective-permute-done.15.rest_0_
  61.0 1.3 %last.1 = (f32[1152,128]{1,0:T(8,128)}, f32[576,128]{1,0:T(8,128)}, f32[576,128]{1,0:T(8,128)}) custom-call(s32[2]{0:T(128)S(1)} %pad_add_fusion.core, bf16[576,128]{1,0:T(8,128)(2,1)S(1)} %collective-permute-done.15.rest_0_, f32[1152,128]{1,0:T(8,128)} %get-tuple-element.76.rest_1_, ...), custom_call_target="tpu_custom_call", output_to_operand_aliasing={{0}: (2, {}), {1}: (3, {}), {2}: (4, {})} | custom-call | flops 1000000 | bytes 100000 | tf_op jit(solution)/shard_map/last/pallas_call | solution.py:380
  (26 shorter events, 0.3 us)
Async XLA Ops:
  0.6 1.0 %copy-start = (bf16[64,4,512]{2,1,0:T(4,128)(2,1)S(1)}, bf16[64,4,512]{2,1,0:T(4,128)(2,1)}, u32[]{:S(2)}) copy-start(bf16[64,4,512]{2,1,0:T(4,128)(2,1)} %param.6) | copy-start | bytes 786436
  0.6 2.0 %copy-start.1 = (bf16[3,3,128,128]{3,2,1,0:T(8,128)(2,1)S(1)}, bf16[3,3,128,128]{3,2,1,0:T(8,128)(2,1)}, u32[]{:S(2)}) copy-start(bf16[3,3,128,128]{3,2,1,0:T(8,128)(2,1)} %param.9) | copy-start | bytes 884740
  0.7 1.4 %copy-start.2 = (bf16[3,3,64,128]{3,2,1,0:T(8,128)(2,1)S(1)}, bf16[3,3,64,128]{3,2,1,0:T(8,128)(2,1)}, u32[]{:S(2)}) copy-start(bf16[3,3,64,128]{3,2,1,0:T(8,128)(2,1)} %param.7) | copy-start | bytes 442372
  0.7 2.0 %copy-start.4 = (bf16[128,2,256]{2,1,0:T(2,128)(2,1)S(1)}, bf16[128,2,256]{2,1,0:T(2,128)(2,1)}, u32[]{:S(2)}) copy-start(bf16[128,2,256]{2,1,0:T(2,128)(2,1)} %param.10) | copy-start | bytes 393220
  2.1 8.2 %copy-start.3 = (bf16[3,3,64,128]{3,2,1,0:T(8,128)(2,1)S(1)}, bf16[3,3,64,128]{3,2,1,0:T(8,128)(2,1)}, u32[]{:S(2)}) copy-start(bf16[3,3,64,128]{3,2,1,0:T(8,128)(2,1)} %param.8) | copy-start | bytes 442372
  2.1 8.2 %collective-permute-start.2 = (bf16[576,128]{1,0:T(8,128)(2,1)S(1)}, bf16[576,128]{1,0:T(8,128)(2,1)S(1)}, u32[]{:S(2)}, u32[]{:S(2)}) collective-permute-start(bf16[576,128]{1,0:T(8,128)(2,1)S(1)} %bitcast.34), channel_id=1, source_target_pairs={{0,1},{1,0},{2,3},{3,2},{4,5},{5,4},{6,7},{7,6},{8,9},{9,8},{10,11... | collective-permute-start | bytes 442376 | tf_op jit(solution)/shard_map/ppermute | solution.py:404
  2.6 9.0 %collective-permute-start.4 = (bf16[1152,128]{1,0:T(8,128)(2,1)S(1)}, bf16[1152,128]{1,0:T(8,128)(2,1)S(1)}, u32[]{:S(2)}, u32[]{:S(2)}) collective-permute-start(bf16[1152,128]{1,0:T(8,128)(2,1)S(1)} %bitcast.32), channel_id=1, source_target_pairs={{0,1},{1,0},{2,3},{3,2},{4,5},{5,4},{6,7},{7,6},{8,9},{9,8},{10,11... | collective-permute-start | bytes 884744 | tf_op jit(solution)/shard_map/ppermute | solution.py:404
  3.0 8.7 %collective-permute-start.1 = (bf16[6,64,512]{2,1,0:T(8,128)(2,1)S(1)}, bf16[6,64,512]{2,1,0:T(8,128)(2,1)S(1)}, u32[]{:S(2)}, u32[]{:S(2)}) collective-permute-start(bf16[6,64,512]{2,1,0:T(8,128)(2,1)S(1)} %maximum_maximum_fusion.own), channel_id=1, source_target_pairs={{0,1},{1,0},{2,3},{3,2},{4,5},{5,4},{6,7},{7,6},{8,9},{9,8},{10,11... | collective-permute-start | bytes 1179656 | tf_op jit(solution)/shard_map/ppermute | solution.py:404
  3.5 14.4 %collective-permute-start = (bf16[4,64,512]{2,1,0:T(8,128)(2,1)S(1)}, bf16[4,64,512]{2,1,0:T(8,128)(2,1)S(1)}, u32[]{:S(2)}, u32[]{:S(2)}) collective-permute-start(bf16[4,64,512]{2,1,0:T(8,128)(2,1)S(1)} %pad_maximum_fusion.1), channel_id=1, source_target_pairs={{0,2},{2,4},{4,6},{6,8},{8,10},{10,12},{12,14},{14,16},{16,18},{18... | collective-permute-start | bytes 786440 | tf_op jit(solution)/shard_map/ppermute | solution.py:423
  6.2 13.7 %collective-permute-start.5 = (bf16[4,64,512]{2,1,0:T(8,128)(2,1)S(1)}, bf16[4,64,512]{2,1,0:T(8,128)(2,1)S(1)}, u32[]{:S(2)}, u32[]{:S(2)}) collective-permute-start(bf16[4,64,512]{2,1,0:T(8,128)(2,1)S(1)} %fusion.5), channel_id=1, source_target_pairs={{2,0},{4,2},{6,4},{8,6},{10,8},{12,10},{14,12},{16,14},{18,16},{20... | collective-permute-start | bytes 786440 | tf_op jit(solution)/shard_map/ppermute | solution.py:424
  10.2 1.4 %collective-permute-start.3 = (bf16[576,128]{1,0:T(8,128)(2,1)S(1)}, bf16[576,128]{1,0:T(8,128)(2,1)S(1)}, u32[]{:S(2)}, u32[]{:S(2)}) collective-permute-start(bf16[576,128]{1,0:T(8,128)(2,1)S(1)} %bitcast.36), channel_id=1, source_target_pairs={{0,1},{1,0},{2,3},{3,2},{4,5},{5,4},{6,7},{7,6},{8,9},{9,8},{10,11... | collective-permute-start | bytes 442376 | tf_op jit(solution)/shard_map/ppermute | solution.py:404
  17.9 2.6 %collective-permute-start.6 = (bf16[4,64,512]{2,1,0:T(8,128)(2,1)S(1)}, bf16[4,64,512]{2,1,0:T(8,128)(2,1)S(1)}, u32[]{:S(2)}, u32[]{:S(2)}) collective-permute-start(bf16[4,64,512]{2,1,0:T(8,128)(2,1)S(1)} %collective-permute-done.around), channel_id=1, source_target_pairs={{0,1},{1,0},{2,3},{3,2},{4,5},{5,4},{6,7},{7,6},{8,9},{9,8},{10,11... | collective-permute-start | bytes 786440 | tf_op jit(solution)/shard_map/ppermute | solution.py:404
  19.9 1.5 %collective-permute-start.7 = (bf16[4,64,512]{2,1,0:T(8,128)(2,1)S(1)}, bf16[4,64,512]{2,1,0:T(8,128)(2,1)S(1)}, u32[]{:S(2)}, u32[]{:S(2)}) collective-permute-start(bf16[4,64,512]{2,1,0:T(8,128)(2,1)S(1)} %collective-permute-done.5.around), channel_id=1, source_target_pairs={{0,1},{1,0},{2,3},{3,2},{4,5},{5,4},{6,7},{7,6},{8,9},{9,8},{10,11... | collective-permute-start | bytes 786440 | tf_op jit(solution)/shard_map/ppermute | solution.py:404
  28.2 6.5 %collective-permute-start.8 = (bf16[576,128]{1,0:T(8,128)(2,1)S(1)}, bf16[576,128]{1,0:T(8,128)(2,1)S(1)}, u32[]{:S(2)}, u32[]{:S(2)}) collective-permute-start(bf16[576,128]{1,0:T(8,128)(2,1)S(1)} %get-tuple-element.65), channel_id=1, source_target_pairs={{0,2},{2,0},{4,6},{6,4},{8,10},{10,8},{12,14},{14,12},{16,18},{18,... | collective-permute-start | bytes 442376 | tf_op jit(solution)/shard_map/ppermute | solution.py:407
  29.8 7.0 %collective-permute-start.9 = (bf16[576,128]{1,0:T(8,128)(2,1)S(1)}, bf16[576,128]{1,0:T(8,128)(2,1)S(1)}, u32[]{:S(2)}, u32[]{:S(2)}) collective-permute-start(bf16[576,128]{1,0:T(8,128)(2,1)S(1)} %get-tuple-element.66), channel_id=1, source_target_pairs={{0,4},{2,6},{4,0},{6,2},{8,12},{10,14},{12,8},{14,10},{16,20},{18,... | collective-permute-start | bytes 442376 | tf_op jit(solution)/shard_map/ppermute | solution.py:407
  30.2 8.5 %collective-permute-start.10 = (bf16[576,128]{1,0:T(8,128)(2,1)S(1)}, bf16[576,128]{1,0:T(8,128)(2,1)S(1)}, u32[]{:S(2)}, u32[]{:S(2)}) collective-permute-start(bf16[576,128]{1,0:T(8,128)(2,1)S(1)} %get-tuple-element.67), channel_id=1, source_target_pairs={{0,6},{2,4},{4,2},{6,0},{8,14},{10,12},{12,10},{14,8},{16,22},{18,... | collective-permute-start | bytes 442376 | tf_op jit(solution)/shard_map/ppermute | solution.py:407
  38.8 5.2 %collective-permute-start.11 = (bf16[576,128]{1,0:T(8,128)(2,1)S(1)}, bf16[576,128]{1,0:T(8,128)(2,1)S(1)}, u32[]{:S(2)}, u32[]{:S(2)}) collective-permute-start(bf16[576,128]{1,0:T(8,128)(2,1)S(1)} %sum.3.refs_0_), channel_id=1, source_target_pairs={{0,8},{2,10},{4,12},{6,14},{8,0},{10,2},{12,4},{14,6},{16,24},{18,... | collective-permute-start | bytes 442376 | tf_op jit(solution)/shard_map/ppermute | solution.py:407
  44.0 8.7 %collective-permute-start.14 = (bf16[576,128]{1,0:T(8,128)(2,1)S(1)}, bf16[576,128]{1,0:T(8,128)(2,1)S(1)}, u32[]{:S(2)}, u32[]{:S(2)}) collective-permute-start(bf16[576,128]{1,0:T(8,128)(2,1)S(1)} %sum.4.refs_0_), channel_id=1, source_target_pairs={{0,16},{2,18},{4,20},{6,22},{8,24},{10,26},{12,28},{14,30},{16,0},... | collective-permute-start | bytes 442376 | tf_op jit(solution)/shard_map/ppermute | solution.py:407
  47.5 8.8 %collective-permute-start.13 = (bf16[64,512]{1,0:T(8,128)(2,1)S(1)}, bf16[64,512]{1,0:T(8,128)(2,1)S(1)}, u32[]{:S(2)}, u32[]{:S(2)}) collective-permute-start(bf16[64,512]{1,0:T(8,128)(2,1)S(1)} %get-tuple-element.91), channel_id=1, source_target_pairs={{2,0},{4,2},{6,4},{8,6},{10,8},{12,10},{14,12},{16,14},{18,16},{20... | collective-permute-start | bytes 196616 | tf_op jit(solution)/shard_map/ppermute | solution.py:484
  49.6 8.1 %collective-permute-start.12 = (bf16[64,512]{1,0:T(8,128)(2,1)S(1)}, bf16[64,512]{1,0:T(8,128)(2,1)S(1)}, u32[]{:S(2)}, u32[]{:S(2)}) collective-permute-start(bf16[64,512]{1,0:T(8,128)(2,1)S(1)} %get-tuple-element.90), channel_id=1, source_target_pairs={{0,2},{2,4},{4,6},{6,8},{8,10},{10,12},{12,14},{14,16},{16,18},{18... | collective-permute-start | bytes 196616 | tf_op jit(solution)/shard_map/ppermute | solution.py:485
  52.7 6.5 %collective-permute-start.17 = (bf16[576,128]{1,0:T(8,128)(2,1)S(1)}, bf16[576,128]{1,0:T(8,128)(2,1)S(1)}, u32[]{:S(2)}, u32[]{:S(2)}) collective-permute-start(bf16[576,128]{1,0:T(8,128)(2,1)S(1)} %sum.5.rest_0_), channel_id=1, source_target_pairs={{0,4},{2,6},{4,0},{6,2},{8,12},{10,14},{12,8},{14,10},{16,20},{18,... | collective-permute-start | bytes 442376 | tf_op jit(solution)/shard_map/ppermute | solution.py:407
  52.8 6.4 %collective-permute-start.16 = (bf16[576,128]{1,0:T(8,128)(2,1)S(1)}, bf16[576,128]{1,0:T(8,128)(2,1)S(1)}, u32[]{:S(2)}, u32[]{:S(2)}) collective-permute-start(bf16[576,128]{1,0:T(8,128)(2,1)S(1)} %sum.5.rest_0_), channel_id=1, source_target_pairs={{0,2},{2,0},{4,6},{6,4},{8,10},{10,8},{12,14},{14,12},{16,18},{18,... | collective-permute-start | bytes 442376 | tf_op jit(solution)/shard_map/ppermute | solution.py:407
  54.4 6.6 %collective-permute-start.15 = (bf16[576,128]{1,0:T(8,128)(2,1)S(1)}, bf16[576,128]{1,0:T(8,128)(2,1)S(1)}, u32[]{:S(2)}, u32[]{:S(2)}) collective-permute-start(bf16[576,128]{1,0:T(8,128)(2,1)S(1)} %sum.5.rest_0_), channel_id=1, source_target_pairs={{0,6},{2,4},{4,2},{6,0},{8,14},{10,12},{12,10},{14,8},{16,22},{18,... | collective-permute-start | bytes 442376 | tf_op jit(solution)/shard_map/ppermute | solution.py:407

commit v2 on v1

--- a/solution.py
+++ b/solution.py
@@ -471,16 +471,17 @@
         aliases={1: 5, 2: 6, 3: 7, 4: 8},
     )
     mine = total(parts[0], *[swapped(part, k) for k, part in enumerate(parts[1:], 1)])
+    mine, td1 = lax.optimization_barrier((mine, td1))
+    main, rims = call(
+        inputs_kernel, "inputs",
+        [((rows, h, cols), F32), ((2, h, cols), BF)], [], 16, td1, wt1,
+    )
     bit = 4
     while bit < tiles:
         if bit * 2 >= tiles:
-            mine, td1 = lax.optimization_barrier((mine, td1))
+            mine, rims = lax.optimization_barrier((mine, rims))
         mine = total(mine, swapped(mine, bit))
         bit *= 2
-    main, rims = call(
-        inputs_kernel, "inputs",
-        [((rows, h, cols), F32), ((2, h, cols), BF)], [], 16, td1, wt1,
-    )
     from_next = lax.ppermute(rims[0], "blk", down)
     from_prev = lax.ppermute(rims[1], "blk", up)
     from_next, _ = lax.optimization_barrier((from_next, mine))

time: 62.4 us -> 62.6 us (level)
    ppermute x8, waiting for transfers between devices: 14 us -> 15 us  [swapped(): return lax.ppermute(piece, 'blk', [(i, i ^ k) for i in range(tiles)])]
    ppermute x1, waiting for transfers between devices: 1.39 us -> 0.52 us  [shards(): from_prev = lax.ppermute(rims[1], 'blk', up)]
where the time goes in v2:
time: 62.6 us; the launch traced here: 62.4 us
  waiting for transfers between devices  22.1 us (35%)
  starting transfers between devices  21.5 us (34%)
  Pallas kernels  14.9 us (24%)
  between operations  1.58 us (3%)
  local copies, waits for them, and re-layouts  1.23 us (2%)
  matrix products  0.98 us (2%)
    ppermute x8, waiting for transfers between devices, swapped(): return lax.ppermute(piece, 'blk', [(i, i ^ k) for i in range(tiles)])  15 us
    pallas_call x10, Pallas kernels, call(): pl.pallas_call(body, out_shape=tuple((jax.ShapeDtypeStruct(shape, kind) f...  14.9 us
    ppermute x8, starting transfers between devices, swapped(): return lax.ppermute(piece, 'blk', [(i, i ^ k) for i in range(tiles)])  11.4 us
    ppermute x1, starting transfers between devices, shards(): after = lax.ppermute(jnp.concatenate([x[:3], u[:1]]), 'blk', down)  4.06 us
    ppermute x1, waiting for transfers between devices, shards(): lax.ppermute(jnp.concatenate([x[rows - 3:], u[rows // 2 - 1:]]), 'blk', up)  3.32 us
    ppermute x1, starting transfers between devices, shards(): lax.ppermute(jnp.concatenate([x[rows - 3:], u[rows // 2 - 1:]]), 'blk', up)  2.63 us
    ppermute x1, starting transfers between devices, shards(): from_next = lax.ppermute(rims[0], 'blk', down)  2.13 us
    ppermute x6, waiting for transfers between devices, across(): return lax.ppermute(piece, 'chan', [(0, 1), (1, 0)])  1.98 us
  transfers between devices with their start and end apart: 18, of which 12 were waited for; matrix products, arithmetic and copies ran while one was open for 3% of the time, Pallas kernels for 11%

profile of v2, /device:TPU:0, one launch (start us, length us, event | category | flops | bytes accessed | tf_op | source)
XLA Modules:
  0.0 62.4 jit_solution(6812790063559014879)
XLA Ops:
  0.6 0.0 copy-start
  1.4 0.2 copy-done
  1.7 0.4 fusion
  2.1 0.0 copy-start.3
  2.1 0.5 collective-permute-start.2
  2.6 0.1 collective-permute-start.4
  2.7 0.2 fusion.2
  3.0 0.5 collective-permute-start.1
  3.5 2.6 %collective-permute-start = (bf16[4,64,512]{2,1,0:T(8,128)(2,1)S(1)}, bf16[4,64,512]{2,1,0:T(8,128)(2,1)S(1)}, u32[]{:S(2)}, u32[]{:S(2)}) collective-permute-start(bf16[4,64,512]{2,1,0:T(8,128)(2,1)S(1)} %pad_maximum_fusion.1), channel_id=1, source_target_pairs={{0,2},{2,4},{4,6},{6,8},{8,10},{10,12},{12,14},{14,16},{16,18},{18... | collective-permute-start | bytes 786440 | tf_op jit(solution)/shard_map/ppermute | solution.py:423
  6.2 4.1 %collective-permute-start.5 = (bf16[4,64,512]{2,1,0:T(8,128)(2,1)S(1)}, bf16[4,64,512]{2,1,0:T(8,128)(2,1)S(1)}, u32[]{:S(2)}, u32[]{:S(2)}) collective-permute-start(bf16[4,64,512]{2,1,0:T(8,128)(2,1)S(1)} %fusion.5), channel_id=1, source_target_pairs={{2,0},{4,2},{6,4},{8,6},{10,8},{12,10},{14,12},{16,14},{18,16},{20... | collective-permute-start | bytes 786440 | tf_op jit(solution)/shard_map/ppermute | solution.py:424
  10.2 0.0 collective-permute-done.2.other1
  10.2 0.2 collective-permute-start.3
  10.4 0.1 pad_add_fusion.core
  10.5 1.1 %collective-permute-done.3.other2 = bf16[576,128]{1,0:T(8,128)(2,1)S(1)} collective-permute-done((bf16[576,128]{1,0:T(8,128)(2,1)S(1)}, bf16[576,128]{1,0:T(8,128)(2,1)S(1)}, u32[]{:S(2)}, u32[]{:S(2)}) %collective-permute-start.3) | collective-permute-done | bytes 147488 | tf_op jit(solution)/shard_map/ppermute | solution.py:404
  11.6 0.0 collective-permute-done.4.other3
  11.6 0.0 collective-permute-done.1.other
  11.6 3.0 %inner.1 = (bf16[256,1536]{1,0:T(8,128)(2,1)S(1)}, bf16[256,1536]{1,0:T(8,128)(2,1)S(1)}, bf16[256,1536]{1,0:T(8,128)(2,1)S(1)}, bf16[128,1536]{1,0:T(8,128)(2,1...) custom-call(s32[2]{0:T(128)S(1)} %pad_add_fusion.core, ...), custom_call_target="tpu_custom_call" | custom-call | flops 1000000 | bytes 100000 | tf_op jit(solution)/shard_map/inner/pallas_call | solution.py:380
  14.6 3.3 %collective-permute-done.around = bf16[4,64,512]{2,1,0:T(8,128)(2,1)S(1)} collective-permute-done((bf16[4,64,512]{2,1,0:T(8,128)(2,1)S(1)}, bf16[4,64,512]{2,1,0:T(8,128)(2,1)S(1)}, u32[]{:S(2)}, u32[]{:S(2)}) %collective-permute-start) | collective-permute-done | bytes 262176 | tf_op jit(solution)/shard_map/ppermute | solution.py:423
  17.9 0.0 collective-permute-start.6
  17.9 0.7 %outer.2 = (bf16[1536,256]{1,0:T(8,128)(2,1)S(1)}, bf16[512,256]{1,0:T(8,128)(2,1)S(1)}) custom-call(s32[2]{0:T(128)S(1)} %pad_add_fusion.core, bf16[4,64,512]{2,1,0:T(8,128)(2,1)S(1)} %collective-permute-done.around), custom_call_target="tpu_custom_call" | custom-call | flops 1000000 | bytes 100000 | tf_op jit(solution)/shard_map/outer/pallas_call | solution.py:380
  18.6 1.3 %collective-permute-done.5.around = bf16[4,64,512]{2,1,0:T(8,128)(2,1)S(1)} collective-permute-done((bf16[4,64,512]{2,1,0:T(8,128)(2,1)S(1)}, bf16[4,64,512]{2,1,0:T(8,128)(2,1)S(1)}, u32[]{:S(2)}, u32[]{:S(2)}) %collective-permute-start.5) | collective-permute-done | bytes 262176 | tf_op jit(solution)/shard_map/ppermute | solution.py:424
  19.9 0.0 collective-permute-start.7
  19.9 0.7 %outer.3 = (bf16[1536,256]{1,0:T(8,128)(2,1)S(1)}, bf16[512,256]{1,0:T(8,128)(2,1)S(1)}) custom-call(s32[2]{0:T(128)S(1)} %pad_add_fusion.core, bf16[4,64,512]{2,1,0:T(8,128)(2,1)S(1)} %collective-permute-done.5.around), custom_call_target="tpu_custom_call" | custom-call | flops 1000000 | bytes 100000 | tf_op jit(solution)/shard_map/outer/pallas_call | solution.py:380
  20.6 0.8 %collective-permute-done.7.after = bf16[4,64,512]{2,1,0:T(8,128)(2,1)S(1)} collective-permute-done((bf16[4,64,512]{2,1,0:T(8,128)(2,1)S(1)}, bf16[4,64,512]{2,1,0:T(8,128)(2,1)S(1)}, u32[]{:S(2)}, u32[]{:S(2)}) %collective-permute-start.7) | collective-permute-done | bytes 262176 | tf_op jit(solution)/shard_map/ppermute | solution.py:404
  21.4 6.8 %main.1 = (bf16[576,128]{1,0:T(8,128)(2,1)S(1)}, bf16[576,128]{1,0:T(8,128)(2,1)S(1)}, bf16[576,128]{1,0:T(8,128)(2,1)S(1)}, bf16[576,128]{1,0:T(8,128)(2,1)S(1)...) custom-call(s32[2]{0:T(128)S(1)} %pad_add_fusion.core, ...), custom_call_target="tpu_custom_call", output_to_operand_aliasing={{5}: (1, {}), {6}: (2, {}), {7}: (3, {}), {8}: (4, {})} | custom-call | flops 1000000 | bytes 100000 | tf_op jit(solution)/shard_map/main/pallas_call | solution.py:380
  28.2 1.6 %collective-permute-start.8 = (bf16[576,128]{1,0:T(8,128)(2,1)S(1)}, bf16[576,128]{1,0:T(8,128)(2,1)S(1)}, u32[]{:S(2)}, u32[]{:S(2)}) collective-permute-start(bf16[576,128]{1,0:T(8,128)(2,1)S(1)} %get-tuple-element.67), channel_id=1, source_target_pairs={{0,2},{2,0},{4,6},{6,4},{8,10},{10,8},{12,14},{14,12},{16,18},{18,... | collective-permute-start | bytes 442376 | tf_op jit(solution)/shard_map/ppermute | solution.py:407
  29.8 0.4 collective-permute-start.9
  30.2 1.6 %collective-permute-start.10 = (bf16[576,128]{1,0:T(8,128)(2,1)S(1)}, bf16[576,128]{1,0:T(8,128)(2,1)S(1)}, u32[]{:S(2)}, u32[]{:S(2)}) collective-permute-start(bf16[576,128]{1,0:T(8,128)(2,1)S(1)} %get-tuple-element.69), channel_id=1, source_target_pairs={{0,6},{2,4},{4,2},{6,0},{8,14},{10,12},{12,10},{14,8},{16,22},{18,... | collective-permute-start | bytes 442376 | tf_op jit(solution)/shard_map/ppermute | solution.py:407
  31.7 2.9 %collective-permute-done.8.refs_1_ = bf16[576,128]{1,0:T(8,128)(2,1)S(1)} collective-permute-done((bf16[576,128]{1,0:T(8,128)(2,1)S(1)}, bf16[576,128]{1,0:T(8,128)(2,1)S(1)}, u32[]{:S(2)}, u32[]{:S(2)}) %collective-permute-start.8) | collective-permute-done | bytes 147488 | tf_op jit(solution)/shard_map/ppermute | solution.py:407
  34.7 2.1 %collective-permute-done.9.refs_2_ = bf16[576,128]{1,0:T(8,128)(2,1)S(1)} collective-permute-done((bf16[576,128]{1,0:T(8,128)(2,1)S(1)}, bf16[576,128]{1,0:T(8,128)(2,1)S(1)}, u32[]{:S(2)}, u32[]{:S(2)}) %collective-permute-start.9) | collective-permute-done | bytes 147488 | tf_op jit(solution)/shard_map/ppermute | solution.py:407
  36.8 1.9 %collective-permute-done.10.refs_3_ = bf16[576,128]{1,0:T(8,128)(2,1)S(1)} collective-permute-done((bf16[576,128]{1,0:T(8,128)(2,1)S(1)}, bf16[576,128]{1,0:T(8,128)(2,1)S(1)}, u32[]{:S(2)}, u32[]{:S(2)}) %collective-permute-start.10) | collective-permute-done | bytes 147488 | tf_op jit(solution)/shard_map/ppermute | solution.py:407
  38.7 0.1 sum.3.refs_0_
  38.8 1.6 %collective-permute-start.11 = (bf16[576,128]{1,0:T(8,128)(2,1)S(1)}, bf16[576,128]{1,0:T(8,128)(2,1)S(1)}, u32[]{:S(2)}, u32[]{:S(2)}) collective-permute-start(bf16[576,128]{1,0:T(8,128)(2,1)S(1)} %sum.3.refs_0_), channel_id=1, source_target_pairs={{0,8},{2,10},{4,12},{6,14},{8,0},{10,2},{12,4},{14,6},{16,24},{18,... | collective-permute-start | bytes 442376 | tf_op jit(solution)/shard_map/ppermute | solution.py:407
  40.4 0.8 %inputs.1 = (f32[4,64,512]{2,1,0:T(8,128)S(1)}, bf16[2,64,512]{2,1,0:T(8,128)(2,1)S(1)}) custom-call(bf16[4096,256]{1,0:T(8,128)(2,1)S(1)} %get-tuple-element.71.td1, bf16[128,1536]{1,0:T(8,128)(2,1)S(1)} %get-tuple-element.72.wt1), custom_call_target="tpu_custom_call" | custom-call | flops 1000000 | bytes 100000 | tf_op jit(solution)/shard_map/inputs/pallas_call | solution.py:380
  41.2 2.8 %collective-permute-done.11.refs_1_ = bf16[576,128]{1,0:T(8,128)(2,1)S(1)} collective-permute-done((bf16[576,128]{1,0:T(8,128)(2,1)S(1)}, bf16[576,128]{1,0:T(8,128)(2,1)S(1)}, u32[]{:S(2)}, u32[]{:S(2)}) %collective-permute-start.11) | collective-permute-done | bytes 147488 | tf_op jit(solution)/shard_map/ppermute | solution.py:407
  44.0 2.7 %collective-permute-start.14 = (bf16[576,128]{1,0:T(8,128)(2,1)S(1)}, bf16[576,128]{1,0:T(8,128)(2,1)S(1)}, u32[]{:S(2)}, u32[]{:S(2)}) collective-permute-start(bf16[576,128]{1,0:T(8,128)(2,1)S(1)} %sum.4.refs_0_), channel_id=1, source_target_pairs={{0,16},{2,18},{4,20},{6,22},{8,24},{10,26},{12,28},{14,30},{16,0},... | collective-permute-start | bytes 442376 | tf_op jit(solution)/shard_map/ppermute | solution.py:407
  46.7 2.1 %collective-permute-start.13 = (bf16[64,512]{1,0:T(8,128)(2,1)S(1)}, bf16[64,512]{1,0:T(8,128)(2,1)S(1)}, u32[]{:S(2)}, u32[]{:S(2)}) collective-permute-start(bf16[64,512]{1,0:T(8,128)(2,1)S(1)} %get-tuple-element.95), channel_id=1, source_target_pairs={{2,0},{4,2},{6,4},{8,6},{10,8},{12,10},{14,12},{16,14},{18,16},{20... | collective-permute-start | bytes 196616 | tf_op jit(solution)/shard_map/ppermute | solution.py:485
  48.9 3.9 %collective-permute-done.14.refs_1_ = bf16[576,128]{1,0:T(8,128)(2,1)S(1)} collective-permute-done((bf16[576,128]{1,0:T(8,128)(2,1)S(1)}, bf16[576,128]{1,0:T(8,128)(2,1)S(1)}, u32[]{:S(2)}, u32[]{:S(2)}) %collective-permute-start.14) | collective-permute-done | bytes 147488 | tf_op jit(solution)/shard_map/ppermute | solution.py:407
  52.8 0.1 collective-permute-start.17
  52.8 2.3 %collective-permute-start.16 = (bf16[576,128]{1,0:T(8,128)(2,1)S(1)}, bf16[576,128]{1,0:T(8,128)(2,1)S(1)}, u32[]{:S(2)}, u32[]{:S(2)}) collective-permute-start(bf16[576,128]{1,0:T(8,128)(2,1)S(1)} %sum.5.rest_0_), channel_id=1, source_target_pairs={{0,2},{2,0},{4,6},{6,4},{8,10},{10,8},{12,14},{14,12},{16,18},{18,... | collective-permute-start | bytes 442376 | tf_op jit(solution)/shard_map/ppermute | solution.py:407
  55.1 1.2 %collective-permute-start.15 = (bf16[576,128]{1,0:T(8,128)(2,1)S(1)}, bf16[576,128]{1,0:T(8,128)(2,1)S(1)}, u32[]{:S(2)}, u32[]{:S(2)}) collective-permute-start(bf16[576,128]{1,0:T(8,128)(2,1)S(1)} %sum.5.rest_0_), channel_id=1, source_target_pairs={{0,6},{2,4},{4,2},{6,0},{8,14},{10,12},{12,10},{14,8},{16,22},{18,... | collective-permute-start | bytes 442376 | tf_op jit(solution)/shard_map/ppermute | solution.py:407
  56.3 0.5 collective-permute-done.12
  56.9 0.4 fusion.1
  57.3 0.9 %copy.19 = bf16[64,4,512]{2,1,0:T(4,128)(2,1)} copy(bf16[64,4,512]{2,0,1:T(8,128)(2,1)S(1)} %fusion.1) | data formatting | bytes 524288
  58.2 1.0 %collective-permute-done.17.rest_2_ = bf16[576,128]{1,0:T(8,128)(2,1)S(1)} collective-permute-done((bf16[576,128]{1,0:T(8,128)(2,1)S(1)}, bf16[576,128]{1,0:T(8,128)(2,1)S(1)}, u32[]{:S(2)}, u32[]{:S(2)}) %collective-permute-start.17) | collective-permute-done | bytes 147488 | tf_op jit(solution)/shard_map/ppermute | solution.py:407
  59.2 1.5 %most.1 = (f32[1152,128]{1,0:T(8,128)}, f32[576,128]{1,0:T(8,128)}, f32[576,128]{1,0:T(8,128)}) custom-call(s32[2]{0:T(128)S(1)} %pad_add_fusion.core, bf16[576,128]{1,0:T(8,128)(2,1)S(1)} %sum.5.rest_0_, bf16[576,128]{1,0:T(8,128)(2,1)S(1)} %collective-permute-done.16.rest_1_, bf16[576,128]{1,0:T(8,128)(2,1)S(1)} %collective-permute-done.17.rest_2_), custom_call_target="tpu_custom_call" | custom-call | flops 1000000 | bytes 100000 | tf_op jit(solution)/shard_map/most/pallas_call | solution.py:380
  60.7 0.4 collective-permute-done.15.rest_0_
  61.1 1.3 %last.1 = (f32[1152,128]{1,0:T(8,128)}, f32[576,128]{1,0:T(8,128)}, f32[576,128]{1,0:T(8,128)}) custom-call(s32[2]{0:T(128)S(1)} %pad_add_fusion.core, bf16[576,128]{1,0:T(8,128)(2,1)S(1)} %collective-permute-done.15.rest_0_, f32[1152,128]{1,0:T(8,128)} %get-tuple-element.80.rest_1_, ...), custom_call_target="tpu_custom_call", output_to_operand_aliasing={{0}: (2, {}), {1}: (3, {}), {2}: (4, {})} | custom-call | flops 1000000 | bytes 100000 | tf_op jit(solution)/shard_map/last/pallas_call | solution.py:380
  (26 shorter events, 0.3 us)
Async XLA Ops:
  0.6 1.0 %copy-start = (bf16[64,4,512]{2,1,0:T(4,128)(2,1)S(1)}, bf16[64,4,512]{2,1,0:T(4,128)(2,1)}, u32[]{:S(2)}) copy-start(bf16[64,4,512]{2,1,0:T(4,128)(2,1)} %param.6) | copy-start | bytes 786436
  0.6 2.0 %copy-start.1 = (bf16[3,3,128,128]{3,2,1,0:T(8,128)(2,1)S(1)}, bf16[3,3,128,128]{3,2,1,0:T(8,128)(2,1)}, u32[]{:S(2)}) copy-start(bf16[3,3,128,128]{3,2,1,0:T(8,128)(2,1)} %param.9) | copy-start | bytes 884740
  0.7 1.4 %copy-start.2 = (bf16[3,3,64,128]{3,2,1,0:T(8,128)(2,1)S(1)}, bf16[3,3,64,128]{3,2,1,0:T(8,128)(2,1)}, u32[]{:S(2)}) copy-start(bf16[3,3,64,128]{3,2,1,0:T(8,128)(2,1)} %param.7) | copy-start | bytes 442372
  0.7 2.0 %copy-start.4 = (bf16[128,2,256]{2,1,0:T(2,128)(2,1)S(1)}, bf16[128,2,256]{2,1,0:T(2,128)(2,1)}, u32[]{:S(2)}) copy-start(bf16[128,2,256]{2,1,0:T(2,128)(2,1)} %param.10) | copy-start | bytes 393220
  2.1 8.2 %copy-start.3 = (bf16[3,3,64,128]{3,2,1,0:T(8,128)(2,1)S(1)}, bf16[3,3,64,128]{3,2,1,0:T(8,128)(2,1)}, u32[]{:S(2)}) copy-start(bf16[3,3,64,128]{3,2,1,0:T(8,128)(2,1)} %param.8) | copy-start | bytes 442372
  2.1 8.2 %collective-permute-start.2 = (bf16[576,128]{1,0:T(8,128)(2,1)S(1)}, bf16[576,128]{1,0:T(8,128)(2,1)S(1)}, u32[]{:S(2)}, u32[]{:S(2)}) collective-permute-start(bf16[576,128]{1,0:T(8,128)(2,1)S(1)} %bitcast.34), channel_id=1, source_target_pairs={{0,1},{1,0},{2,3},{3,2},{4,5},{5,4},{6,7},{7,6},{8,9},{9,8},{10,11... | collective-permute-start | bytes 442376 | tf_op jit(solution)/shard_map/ppermute | solution.py:404
  2.6 9.0 %collective-permute-start.4 = (bf16[1152,128]{1,0:T(8,128)(2,1)S(1)}, bf16[1152,128]{1,0:T(8,128)(2,1)S(1)}, u32[]{:S(2)}, u32[]{:S(2)}) collective-permute-start(bf16[1152,128]{1,0:T(8,128)(2,1)S(1)} %bitcast.32), channel_id=1, source_target_pairs={{0,1},{1,0},{2,3},{3,2},{4,5},{5,4},{6,7},{7,6},{8,9},{9,8},{10,11... | collective-permute-start | bytes 884744 | tf_op jit(solution)/shard_map/ppermute | solution.py:404
  3.0 8.7 %collective-permute-start.1 = (bf16[6,64,512]{2,1,0:T(8,128)(2,1)S(1)}, bf16[6,64,512]{2,1,0:T(8,128)(2,1)S(1)}, u32[]{:S(2)}, u32[]{:S(2)}) collective-permute-start(bf16[6,64,512]{2,1,0:T(8,128)(2,1)S(1)} %maximum_maximum_fusion.own), channel_id=1, source_target_pairs={{0,1},{1,0},{2,3},{3,2},{4,5},{5,4},{6,7},{7,6},{8,9},{9,8},{10,11... | collective-permute-start | bytes 1179656 | tf_op jit(solution)/shard_map/ppermute | solution.py:404
  3.5 14.4 %collective-permute-start = (bf16[4,64,512]{2,1,0:T(8,128)(2,1)S(1)}, bf16[4,64,512]{2,1,0:T(8,128)(2,1)S(1)}, u32[]{:S(2)}, u32[]{:S(2)}) collective-permute-start(bf16[4,64,512]{2,1,0:T(8,128)(2,1)S(1)} %pad_maximum_fusion.1), channel_id=1, source_target_pairs={{0,2},{2,4},{4,6},{6,8},{8,10},{10,12},{12,14},{14,16},{16,18},{18... | collective-permute-start | bytes 786440 | tf_op jit(solution)/shard_map/ppermute | solution.py:423
  6.2 13.7 %collective-permute-start.5 = (bf16[4,64,512]{2,1,0:T(8,128)(2,1)S(1)}, bf16[4,64,512]{2,1,0:T(8,128)(2,1)S(1)}, u32[]{:S(2)}, u32[]{:S(2)}) collective-permute-start(bf16[4,64,512]{2,1,0:T(8,128)(2,1)S(1)} %fusion.5), channel_id=1, source_target_pairs={{2,0},{4,2},{6,4},{8,6},{10,8},{12,10},{14,12},{16,14},{18,16},{20... | collective-permute-start | bytes 786440 | tf_op jit(solution)/shard_map/ppermute | solution.py:424
  10.2 1.4 %collective-permute-start.3 = (bf16[576,128]{1,0:T(8,128)(2,1)S(1)}, bf16[576,128]{1,0:T(8,128)(2,1)S(1)}, u32[]{:S(2)}, u32[]{:S(2)}) collective-permute-start(bf16[576,128]{1,0:T(8,128)(2,1)S(1)} %bitcast.36), channel_id=1, source_target_pairs={{0,1},{1,0},{2,3},{3,2},{4,5},{5,4},{6,7},{7,6},{8,9},{9,8},{10,11... | collective-permute-start | bytes 442376 | tf_op jit(solution)/shard_map/ppermute | solution.py:404
  17.9 2.6 %collective-permute-start.6 = (bf16[4,64,512]{2,1,0:T(8,128)(2,1)S(1)}, bf16[4,64,512]{2,1,0:T(8,128)(2,1)S(1)}, u32[]{:S(2)}, u32[]{:S(2)}) collective-permute-start(bf16[4,64,512]{2,1,0:T(8,128)(2,1)S(1)} %collective-permute-done.around), channel_id=1, source_target_pairs={{0,1},{1,0},{2,3},{3,2},{4,5},{5,4},{6,7},{7,6},{8,9},{9,8},{10,11... | collective-permute-start | bytes 786440 | tf_op jit(solution)/shard_map/ppermute | solution.py:404
  19.9 1.5 %collective-permute-start.7 = (bf16[4,64,512]{2,1,0:T(8,128)(2,1)S(1)}, bf16[4,64,512]{2,1,0:T(8,128)(2,1)S(1)}, u32[]{:S(2)}, u32[]{:S(2)}) collective-permute-start(bf16[4,64,512]{2,1,0:T(8,128)(2,1)S(1)} %collective-permute-done.5.around), channel_id=1, source_target_pairs={{0,1},{1,0},{2,3},{3,2},{4,5},{5,4},{6,7},{7,6},{8,9},{9,8},{10,11... | collective-permute-start | bytes 786440 | tf_op jit(solution)/shard_map/ppermute | solution.py:404
  28.2 6.5 %collective-permute-start.8 = (bf16[576,128]{1,0:T(8,128)(2,1)S(1)}, bf16[576,128]{1,0:T(8,128)(2,1)S(1)}, u32[]{:S(2)}, u32[]{:S(2)}) collective-permute-start(bf16[576,128]{1,0:T(8,128)(2,1)S(1)} %get-tuple-element.67), channel_id=1, source_target_pairs={{0,2},{2,0},{4,6},{6,4},{8,10},{10,8},{12,14},{14,12},{16,18},{18,... | collective-permute-start | bytes 442376 | tf_op jit(solution)/shard_map/ppermute | solution.py:407
  29.8 7.0 %collective-permute-start.9 = (bf16[576,128]{1,0:T(8,128)(2,1)S(1)}, bf16[576,128]{1,0:T(8,128)(2,1)S(1)}, u32[]{:S(2)}, u32[]{:S(2)}) collective-permute-start(bf16[576,128]{1,0:T(8,128)(2,1)S(1)} %get-tuple-element.68), channel_id=1, source_target_pairs={{0,4},{2,6},{4,0},{6,2},{8,12},{10,14},{12,8},{14,10},{16,20},{18,... | collective-permute-start | bytes 442376 | tf_op jit(solution)/shard_map/ppermute | solution.py:407
  30.2 8.5 %collective-permute-start.10 = (bf16[576,128]{1,0:T(8,128)(2,1)S(1)}, bf16[576,128]{1,0:T(8,128)(2,1)S(1)}, u32[]{:S(2)}, u32[]{:S(2)}) collective-permute-start(bf16[576,128]{1,0:T(8,128)(2,1)S(1)} %get-tuple-element.69), channel_id=1, source_target_pairs={{0,6},{2,4},{4,2},{6,0},{8,14},{10,12},{12,10},{14,8},{16,22},{18,... | collective-permute-start | bytes 442376 | tf_op jit(solution)/shard_map/ppermute | solution.py:407
  38.8 5.2 %collective-permute-start.11 = (bf16[576,128]{1,0:T(8,128)(2,1)S(1)}, bf16[576,128]{1,0:T(8,128)(2,1)S(1)}, u32[]{:S(2)}, u32[]{:S(2)}) collective-permute-start(bf16[576,128]{1,0:T(8,128)(2,1)S(1)} %sum.3.refs_0_), channel_id=1, source_target_pairs={{0,8},{2,10},{4,12},{6,14},{8,0},{10,2},{12,4},{14,6},{16,24},{18,... | collective-permute-start | bytes 442376 | tf_op jit(solution)/shard_map/ppermute | solution.py:407
  44.0 8.7 %collective-permute-start.14 = (bf16[576,128]{1,0:T(8,128)(2,1)S(1)}, bf16[576,128]{1,0:T(8,128)(2,1)S(1)}, u32[]{:S(2)}, u32[]{:S(2)}) collective-permute-start(bf16[576,128]{1,0:T(8,128)(2,1)S(1)} %sum.4.refs_0_), channel_id=1, source_target_pairs={{0,16},{2,18},{4,20},{6,22},{8,24},{10,26},{12,28},{14,30},{16,0},... | collective-permute-start | bytes 442376 | tf_op jit(solution)/shard_map/ppermute | solution.py:407
  46.7 9.6 %collective-permute-start.13 = (bf16[64,512]{1,0:T(8,128)(2,1)S(1)}, bf16[64,512]{1,0:T(8,128)(2,1)S(1)}, u32[]{:S(2)}, u32[]{:S(2)}) collective-permute-start(bf16[64,512]{1,0:T(8,128)(2,1)S(1)} %get-tuple-element.95), channel_id=1, source_target_pairs={{2,0},{4,2},{6,4},{8,6},{10,8},{12,10},{14,12},{16,14},{18,16},{20... | collective-permute-start | bytes 196616 | tf_op jit(solution)/shard_map/ppermute | solution.py:485
  48.8 8.0 %collective-permute-start.12 = (bf16[64,512]{1,0:T(8,128)(2,1)S(1)}, bf16[64,512]{1,0:T(8,128)(2,1)S(1)}, u32[]{:S(2)}, u32[]{:S(2)}) collective-permute-start(bf16[64,512]{1,0:T(8,128)(2,1)S(1)} %get-tuple-element.94), channel_id=1, source_target_pairs={{0,2},{2,4},{4,6},{6,8},{8,10},{10,12},{12,14},{14,16},{16,18},{18... | collective-permute-start | bytes 196616 | tf_op jit(solution)/shard_map/ppermute | solution.py:486
  52.8 6.5 %collective-permute-start.17 = (bf16[576,128]{1,0:T(8,128)(2,1)S(1)}, bf16[576,128]{1,0:T(8,128)(2,1)S(1)}, u32[]{:S(2)}, u32[]{:S(2)}) collective-permute-start(bf16[576,128]{1,0:T(8,128)(2,1)S(1)} %sum.5.rest_0_), channel_id=1, source_target_pairs={{0,4},{2,6},{4,0},{6,2},{8,12},{10,14},{12,8},{14,10},{16,20},{18,... | collective-permute-start | bytes 442376 | tf_op jit(solution)/shard_map/ppermute | solution.py:407
  52.8 6.4 %collective-permute-start.16 = (bf16[576,128]{1,0:T(8,128)(2,1)S(1)}, bf16[576,128]{1,0:T(8,128)(2,1)S(1)}, u32[]{:S(2)}, u32[]{:S(2)}) collective-permute-start(bf16[576,128]{1,0:T(8,128)(2,1)S(1)} %sum.5.rest_0_), channel_id=1, source_target_pairs={{0,2},{2,0},{4,6},{6,4},{8,10},{10,8},{12,14},{14,12},{16,18},{18,... | collective-permute-start | bytes 442376 | tf_op jit(solution)/shard_map/ppermute | solution.py:407
  55.1 6.0 %collective-permute-start.15 = (bf16[576,128]{1,0:T(8,128)(2,1)S(1)}, bf16[576,128]{1,0:T(8,128)(2,1)S(1)}, u32[]{:S(2)}, u32[]{:S(2)}) collective-permute-start(bf16[576,128]{1,0:T(8,128)(2,1)S(1)} %sum.5.rest_0_), channel_id=1, source_target_pairs={{0,6},{2,4},{4,2},{6,0},{8,14},{10,12},{12,10},{14,8},{16,22},{18,... | collective-permute-start | bytes 442376 | tf_op jit(solution)/shard_map/ppermute | solution.py:407
